TPU v7x, 128 devices: a whole 4x4x4 slice. The times are simulated.
128 devices in a mesh: node: 8 (over z_lo, x), local: 16 (over y, z_hi, core).
Axes of the slice: x: 4, y: 4, z: 4 (z_hi: 2, z_lo: 2; z = z_hi * 2 + z_lo), core: 2. Of those that a mesh axis runs over, the one named last changes fastest.
Arguments:
- tokens: bfloat16 [131072, 8192], P(('node', 'local')), may hold values from -24 to 24
- positions: int32 [131072], P(('node', 'local')), may hold values from 0 to 4095
- weight_codes: bfloat16 [8192, 512], P('local'), may hold values from -4 to 4
- weight_scales: float32 [8192, 2], P('local'), may hold values from 0.00390625 to 0.03125
- key_cotangent: bfloat16 [131072, 512], P(('node', 'local')), may hold values from -6 to 6
Outputs:
- keys: bfloat16 [131072, 512], P(('node', 'local'))
- weight_grad: float32 [8192, 512], P(('node', 'local'))
All inputs are finite; a program needn't handle non-finite values.
Results may differ from a plain program's by a relative error of at most 0.0029.
Values may be sent and summed in bfloat16 or wider, within the bound.
No kernel may reach another device: no remote copies, remote signals or barrier semaphores. Data moves between devices by JAX's collectives and lax.ppermute only.
A program may use at most 128 MiB of HBM per device.

v0:
```python
import jax
import jax.numpy as jnp
from jax import lax
from jax.sharding import PartitionSpec as P

HD = 128
BLOCK = 256


def rotation(positions, head):
    half = head // 2
    freq = 10000.0 ** (-(2.0 * jnp.arange(half, dtype=jnp.float32)) / head)
    angle = positions.astype(jnp.float32)[:, None] * freq[None, :]
    return (jnp.cos(angle)[:, None, :], jnp.sin(angle)[:, None, :])


def local(tokens, positions, weight_codes, weight_scales, key_cotangent):
    rows = tokens.shape[0]
    width = weight_codes.shape[1]
    heads = width // HD
    half = HD // 2
    cosine, sine = rotation(positions, HD)
    grads = key_cotangent.astype(jnp.float32).reshape(rows, heads, HD)
    gfirst, gsecond = (grads[..., :half], grads[..., half:])
    back = jnp.concatenate(
        [gfirst * cosine + gsecond * sine, gsecond * cosine - gfirst * sine], axis=-1
    )
    back = back.reshape(rows, width).astype(jnp.bfloat16)
    partial_grad = lax.dot_general(
        tokens, back, (((0,), (0,)), ((), ())), preferred_element_type=jnp.float32
    )
    codes = lax.all_gather(weight_codes, "local", axis=0, tiled=True)
    scales = lax.all_gather(weight_scales.astype(jnp.bfloat16), "local", axis=0, tiled=True).astype(
        jnp.float32
    )
    weight = (codes.astype(jnp.float32) * jnp.repeat(scales, BLOCK, axis=1)).astype(jnp.bfloat16)
    raw = jnp.dot(tokens, weight, preferred_element_type=jnp.float32)
    raw = raw.reshape(rows, heads, HD)
    first, second = (raw[..., :half], raw[..., half:])
    keys = jnp.concatenate(
        [first * cosine - second * sine, second * cosine + first * sine], axis=-1
    )
    keys = keys.reshape(rows, width).astype(jnp.bfloat16)
    n_node = lax.axis_size("node")
    n_local = lax.axis_size("local")
    depth = partial_grad.shape[0]
    shaped = partial_grad.reshape(n_node, depth // n_node, width)
    within = lax.psum_scatter(shaped, "local", scatter_dimension=1, tiled=True)
    across = lax.psum_scatter(within, "node", scatter_dimension=0, tiled=True)
    weight_grad = across.reshape(depth // (n_node * n_local), width)
    return (keys, weight_grad)


def solution(mesh):
    placed = (
        P(("node", "local"), None),
        P(("node", "local")),
        P("local", None),
        P("local", None),
        P(("node", "local"), None),
    )
    return jax.shard_map(
        local,
        mesh=mesh,
        in_specs=placed,
        out_specs=(P(("node", "local"), None), P(("node", "local"), None)),
        check_vma=False,
    )
```

profile of v0, /device:TPU:0, one launch (start us, length us, event | category | flops | bytes accessed | tf_op | source)
XLA Modules:
  0.0 333.5 jit_solution(9526917067307246410)
XLA Ops:
  7.2 0.0 all-gather.2.cloned.1.call-start
  7.2 0.7 all-gather.2.cloned.1.call-update
  7.9 0.0 reduce-scatter.3.cloned.1.call-start
  7.9 0.7 convert_element_type.28
  8.6 0.7 convert_element_type.25
  9.3 25.5 %all_gather.7 = bf16[8192,2]{0,1:T(2,128)(2,1)S(1)} all-gather(bf16[512,2]{0,1:T(2,128)(2,1)S(1)} %convert_element_type.25), channel_id=1, replica_groups=mesh['node'=8,'local'=16] {'local'}, dimensions={0}, use_global_device_ids=true | all-gather | bytes 34816 | tf_op jit(solution)/shard_map/all_gather | solution.py:33
  34.8 2.4 copy.7
  37.2 11.0 %broadcast_in_dim.2 = f32[8192,2,256]{2,1,0:T(2,128)S(1)} broadcast(f32[8192,2]{1,0:T(8,128)} %copy.7), dimensions={0,1} | broadcast | bytes 16842752 | tf_op jit(solution)/shard_map/broadcast_in_dim | solution.py:36
  48.2 0.0 copy-start
  48.2 7.2 %copy.15 = f32[1024,8,2,256]{3,1,2,0:T(8,128)} copy(f32[1024,8,2,256]{3,2,1,0:T(2,128)S(1)} %bitcast.15) | data formatting | bytes 33554432
  55.4 0.0 copy-done
  55.4 0.5 copy.14
  55.9 1.0 multiply_cosine_fusion
  56.9 28.8 %all-gather.2.cloned.1.call-done = bf16[8192,512]{1,0:T(8,128)(2,1)} async-done(((bf16[512,512]{1,0:T(8,128)(2,1)}), bf16[8192,512]{1,0:T(8,128)(2,1)}) %all-gather.2.cloned.1.call-update) | async-done | bytes 8388624 | tf_op jit(solution)/shard_map/all_gather | solution.py:32
  85.7 22.6 %fusion = f32[512,1024]{1,0:T(8,128)S(1)} fusion(bf16[1024,8192]{1,0:T(8,128)(2,1)} %param.5, f32[8192,512]{1,0:T(8,128)} %bitcast.17, bf16[8192,512]{1,0:T(8,128)(2,1)} %all-gather.2.cloned.1.call-done), kind=kOutput, calls=%fused_computation.2 | convolution fusion | flops 8602517504 | bytes 44040192 | tf_op jit(solution)/shard_map/dot_general | solution.py:37
  108.3 0.7 add_convert_fusion
  109.0 0.2 pad_maximum_fusion
  109.3 15.7 %convolution_bitcast_fusion = f32[8192,512]{0,1:T(8,128)} fusion(bf16[1024,512]{0,1:T(8,128)(2,1)S(1)} %bitcast.21, bf16[1024,8192]{1,0:T(8,128)(2,1)} %param.5), kind=kOutput, calls=%fused_computation.1 | convolution fusion | flops 8589934592 | bytes 34603008 | tf_op jit(solution)/shard_map/dot_general | solution.py:29
  124.9 17.4 %copy.13 = f32[8192,512]{1,0:T(8,128)} copy(f32[8192,512]{0,1:T(8,128)} %convolution_bitcast_fusion) | data formatting | bytes 33554432 | tf_op jit(solution)/shard_map/reshape | solution.py:47
  142.4 0.0 reduce-scatter.3.cloned.1.call-update
  142.4 0.0 reduce-scatter.5.cloned.1.call-start
  142.4 144.7 %reduce-scatter.3.cloned.1.call-done = f32[8,64,512]{2,1,0:T(8,128)} async-done(((f32[8,1024,512]{2,1,0:T(8,128)}), f32[8,64,512]{2,1,0:T(8,128)}) %reduce-scatter.3.cloned.1.call-update) | async-done | bytes 1048592 | tf_op jit(solution)/shard_map/reduce_scatter | solution.py:48
  287.1 0.0 reduce-scatter.5.cloned.1.call-update
  287.1 1.3 copy.12
  288.5 38.5 %reduce-scatter.5.cloned.1.call-done = f32[1,64,512]{2,1,0:T(8,128)} async-done(((f32[8,64,512]{2,1,0:T(8,128)}), f32[1,64,512]{2,1,0:T(8,128)}) %reduce-scatter.5.cloned.1.call-update) | async-done | bytes 131088 | tf_op jit(solution)/shard_map/reduce_scatter | solution.py:49
  (1 shorter events, 0.0 us)
Async XLA Ops:
  7.2 78.6 %all-gather.2.cloned.1.call-start = ((), (), s32[]{:S(2)}) async-start(), calls=%async_computation.2 | async-start | bytes 8912896 | tf_op jit(solution)/shard_map/all_gather | solution.py:32
  7.9 279.2 %reduce-scatter.3.cloned.1.call-start = ((), (), s32[]{:S(2)}) async-start(), calls=%async_computation.3 | async-start | bytes 17825792 | tf_op jit(solution)/shard_map/reduce_scatter | solution.py:48
  48.2 7.2 %copy-start = (bf16[1024,512]{1,0:T(8,128)(2,1)S(1)}, bf16[1024,512]{1,0:T(8,128)(2,1)}, u32[]{:S(2)}) copy-start(bf16[1024,512]{1,0:T(8,128)(2,1)} %param.9) | copy-start | bytes 3145732
  142.4 184.6 %reduce-scatter.5.cloned.1.call-start = ((), (), s32[]{:S(2)}) async-start(), calls=%async_computation.4 | async-start | bytes 1179648 | tf_op jit(solution)/shard_map/reduce_scatter | solution.py:49
Sparse Core Ops, SparseCore 0:
  10.4 75.3 all-gather.1
  142.5 144.5 reduce-scatter.2
  290.2 36.7 reduce-scatter.4
where the time goes:
time: 334 us
  waiting for transfers between devices  213 us (64%)
  local copies, waits for them, and re-layouts  39.8 us (12%)
  matrix products  38.3 us (11%)
  blocking collectives  25.5 us (8%)
  between operations  13.8 us (4%)
    reduce_scatter x1, waiting for transfers between devices, local(): within = lax.psum_scatter(shaped, 'local', scatter_dimension=1, tiled=True)  145 us
    reduce_scatter x1, waiting for transfers between devices, local(): across = lax.psum_scatter(within, 'node', scatter_dimension=0, tiled=True)  38.5 us
    all_gather x1, waiting for transfers between devices, local(): codes = lax.all_gather(weight_codes, 'local', axis=0, tiled=True)  28.8 us
    all_gather x1, blocking collectives, local(): lax.all_gather(weight_scales.astype(jnp.bfloat16), 'local', axis=0, tiled...  25.5 us
    dot_general x1, matrix products, local(): raw = jnp.dot(tokens, weight, preferred_element_type=jnp.float32)  22.6 us
    reshape x1, local copies, waits for them, and re-layouts, local(): shaped = partial_grad.reshape(n_node, depth // n_node, width)  17.4 us
    dot_general x1, matrix products, local(): lax.dot_general(tokens, back, (((0,), (0,)), ((), ())), preferred_element...  15.7 us
    broadcast_in_dim x1, local copies, waits for them, and re-layouts, local(): jnp.repeat(scales, BLOCK, axis=1)  11 us
  transfers between devices with their start and end apart: 3, of which 3 were waited for; matrix products, arithmetic and copies ran while one was open for 7% of the time, Pallas kernels for 0%

commit v1 on v0

v1 whole, which is shorter than its diff:
```python
import jax
import jax.numpy as jnp
from jax import lax
from jax.experimental import pallas as pl
from jax.experimental.pallas import tpu as pltpu
from jax.sharding import Mesh, PartitionSpec as P

HD = 128
HALF = 64
BLOCK = 256
BF16 = jnp.bfloat16
F32 = jnp.float32
MIB = 1024 * 1024
BITS = ("zlo", "xhi", "xlo", "yhi", "ylo", "zhi", "core")
LIMIT = 8 * MIB
LARGE = 36 * MIB
VMEM = pl.BlockSpec(memory_space=pltpu.VMEM)
SCALAR = pl.BlockSpec(memory_space=pltpu.SMEM)
NEAR, BACK = (1, 3), (3, 1)


def coordinates(device):
    return (device >> 4) & 3, (device >> 2) & 3, device >> 6, (device >> 1) & 1, device & 1


def side(v, core):
    return v & 1 if core else v >> 1


def quads():
    groups = {}
    for device in range(128):
        x, y, zlo, zhi, core = coordinates(device)
        sides = side(x, core), side(y, core)
        name = core, *(v ^ BACK[core] * s for v, s in zip((x, y), sides))
        groups.setdefault(name, []).append((zlo, *sides, zhi, device))
    return [[member[-1] for member in sorted(members)] for members in groups.values()]


STAY = (0, 0)


def send(value, x=STAY, y=STAY, z=STAY, core=STAY):
    pairs = []
    for src in range(128):
        at_x, at_y, zlo, zhi, at_core = coordinates(src)
        at_z = (2 * zhi + zlo) ^ z[at_core]
        place = ((at_z & 1) << 6) | ((at_x ^ x[at_core]) << 4) | ((at_y ^ y[at_core]) << 2) | ((at_z >> 1) << 1)
        pairs.append((src, place | (at_core ^ core[at_core])))
    return lax.ppermute(value, BITS, pairs)


def held_at(distance, core):
    near = jnp.where(core == 0, 1, 3)
    return jnp.where(distance == 0, 0, jnp.where(distance == 2, 3, jnp.where(distance == near, 1, 2)))


def weight_kernel(at, codes_ref, scales_ref, piece_ref, scaled):
    scales = jnp.concatenate([scales_ref[...]] * 4, axis=0).T
    for block in range(2):
        columns = slice(block * BLOCK, (block + 1) * BLOCK)
        scaled[:, columns] = (codes_ref[:, columns].astype(F32) * scales[:, block : block + 1]).astype(BF16)
    piece_ref[0] = scaled[pl.ds(pl.multiple_of(at[2] * 256, 256), 256)]


def weight_piece(at, codes, scales):
    rows, width = codes.shape
    return pl.pallas_call(
        weight_kernel,
        in_specs=[SCALAR, VMEM, VMEM],
        out_specs=VMEM,
        out_shape=jax.ShapeDtypeStruct((1, rows // 2, width), BF16),
        scratch_shapes=[pltpu.VMEM((rows, width), BF16)],
        compiler_params=pltpu.CompilerParams(vmem_limit_bytes=LIMIT),
        name="weight",
    )(at, codes, scales)


def back_kernel(cotangent_ref, cos_ref, sin_ref, back_ref, cos2_ref, sin2_ref):
    cos = jnp.concatenate([cos_ref[...], cos_ref[...]], axis=0).T
    sin = jnp.concatenate([-sin_ref[...], sin_ref[...]], axis=0).T
    cos2_ref[...] = cos
    sin2_ref[...] = sin
    for head in range(4):
        given = cotangent_ref[:, head * HD : (head + 1) * HD].astype(F32)
        back_ref[:, head * HD : (head + 1) * HD] = (given * cos - pltpu.roll(given, HALF, 1) * sin).astype(BF16)


def back_of(cotangent, cos, sin):
    rows, width = cotangent.shape
    turn = jax.ShapeDtypeStruct((rows, HD), F32)
    return pl.pallas_call(
        back_kernel,
        in_specs=[VMEM] * 3,
        out_specs=[VMEM] * 3,
        out_shape=[jax.ShapeDtypeStruct((rows, width), BF16), turn, turn],
        compiler_params=pltpu.CompilerParams(vmem_limit_bytes=LIMIT),
        name="back",
    )(cotangent, cos, sin)


def grad_kernel(chunk, at, back_ref, tokens_ref, own_ref, sib_ref, kept_ref, arrived):
    x, y, zlo, core = at[0], at[1], at[2], at[4]

    def fetch(i):
        column = pl.multiple_of(((zlo ^ chunk) * 4 + i) * 1024, 1024)
        return pltpu.make_async_copy(tokens_ref.at[:, pl.ds(column, 1024)], kept_ref.at[i], arrived.at[i])

    def place(to, here, holder):
        low, high = (to ^ here) & 1, (to ^ here) >> 1
        return jnp.where(holder == 0, to >> 1, to & 1), high ^ (low & (1 - holder))

    for i in range(4):
        fetch(i).start()
    for i in range(4):
        fetch(i).wait()
        for pair in range(2):
            block = kept_ref[i, :, pair * 512 : (pair + 1) * 512]
            part = lax.dot_general(block, back_ref[...], (((0,), (0,)), ((), ())), preferred_element_type=F32)
            for j in range(4):
                to_y, to_zhi = 2 * pair + j // 2, j % 2
                halves = part[j * 128 : j * 128 + 64], part[j * 128 + 64 : (j + 1) * 128]
                for ref, holder, half in (
                    (own_ref, core, jnp.where(core == 0, halves[0], halves[1])),
                    (sib_ref, 1 - core, jnp.where(core == 0, halves[1], halves[0])),
                ):
                    ref[(*place(i, x, holder), *place(to_y, y, holder), to_zhi)] = half.astype(ref.dtype)


def grad_half(at, back, tokens, chunk):
    rows, width = back.shape
    blocks = (2, 2, 2, 2, 2, 64, width)
    return pl.pallas_call(
        lambda *refs: grad_kernel(chunk, *refs),
        in_specs=[SCALAR, VMEM, pl.BlockSpec(memory_space=pltpu.HBM)],
        out_specs=[VMEM, VMEM],
        out_shape=[
            jax.ShapeDtypeStruct(blocks, F32),
            jax.ShapeDtypeStruct(blocks, BF16),
        ],
        scratch_shapes=[pltpu.VMEM((4, rows, 1024), BF16), pltpu.SemaphoreType.DMA((4,))],
        compiler_params=pltpu.CompilerParams(vmem_limit_bytes=LARGE),
        cost_estimate=pl.CostEstimate(flops=20 * rows * 4096 * width, bytes_accessed=8 * MIB, transcendentals=0),
        name="grad",
    )(at, back, tokens)


def forward_kernel(other, at, tokens_ref, weight_ref, *rest):
    y, zlo, zhi, core = at[1], at[2], at[3], at[4]
    acc, weight, block, arrived, filled = rest[-5:]
    holder = core ^ other

    def fetch(i):
        column = pl.multiple_of((2 * i + holder) * 512, 512)
        return pltpu.make_async_copy(tokens_ref.at[:, pl.ds(column, 512)], block.at[i], arrived.at[i])

    def fill(i, to_zlo):
        from_y = held_at(y ^ (i // 2), holder)
        from_z = held_at((2 * zhi + zlo) ^ (2 * (i % 2) + to_zlo), holder)
        rows = pl.ds(to_zlo * 256, 256)
        return pltpu.make_async_copy(
            weight_ref.at[from_z * 4 + from_y], weight.at[i, rows], filled.at[2 * i + to_zlo]
        )

    for i in range(8):
        fetch(i).start()
        fill(i, 0).start()
        fill(i, 1).start()
    acc[...] = rest[0][...] if other else jnp.zeros_like(acc)

    @pl.loop(0, 8)
    def _(i):
        fetch(i).wait()
        fill(i, 0).wait()
        fill(i, 1).wait()
        acc[...] += jnp.dot(block[i], weight[i], preferred_element_type=F32)

    if other:
        cos_ref, sin_ref, keys_ref = rest[1:4]
        for head in range(4):
            raw = acc[:, head * HD : (head + 1) * HD]
            turned = pltpu.roll(raw, HALF, 1)
            keys_ref[:, head * HD : (head + 1) * HD] = (raw * cos_ref[...] + turned * sin_ref[...]).astype(BF16)


def forward(at, tokens, weight, *rest):
    rows, depth = tokens.shape
    width = weight.shape[-1]
    hbm = pl.BlockSpec(memory_space=pltpu.HBM)
    total = pltpu.VMEM((rows, width), F32)
    return pl.pallas_call(
        lambda *refs: forward_kernel(int(bool(rest)), *refs),
        in_specs=[SCALAR, hbm, hbm] + [VMEM] * len(rest),
        out_specs=VMEM,
        scratch_shapes=[total] * bool(rest)
        + [
            pltpu.VMEM((8, 512, width), BF16),
            pltpu.VMEM((8, rows, 512), BF16),
            pltpu.SemaphoreType.DMA((8,)),
            pltpu.SemaphoreType.DMA((16,)),
        ],
        out_shape=jax.ShapeDtypeStruct((rows, width), BF16 if rest else F32),
        compiler_params=pltpu.CompilerParams(vmem_limit_bytes=LARGE),
        cost_estimate=pl.CostEstimate(flops=4 * rows * depth * width, bytes_accessed=4 * MIB, transcendentals=0),
        name="forward",
    )(at, tokens, weight, *rest)


def sums_kernel(at, near_ref, near_in_ref, far_ref, far_in_ref, out_ref):
    zlo = at[2]
    for kx in range(2):
        for ky in range(2):
            out_ref[zlo, kx, ky] = (near_ref[kx, 0, ky] + near_in_ref[kx, ky].astype(F32)).astype(BF16)
            out_ref[1 - zlo, kx, ky] = (far_ref[kx, ky, 0] + far_in_ref[kx, ky].astype(F32)).astype(BF16)


def sums(at, near, near_in, far, far_in):
    out = (2, *near_in.shape)
    return pl.pallas_call(
        sums_kernel,
        in_specs=[SCALAR] + [VMEM] * 4,
        out_specs=VMEM,
        out_shape=jax.ShapeDtypeStruct(out, BF16),
        compiler_params=pltpu.CompilerParams(vmem_limit_bytes=LIMIT),
        name="sums",
    )(at, near, near_in, far, far_in)


def local(tokens, positions, weight_codes, weight_scales, key_cotangent):
    x, y, zlo, zhi, core = coordinates(lax.axis_index(BITS))
    at = jnp.stack([x, y, zlo, zhi, core]).astype(jnp.int32)
    tie = lax.optimization_barrier

    weight = weight_piece(at, weight_codes, weight_scales.T)
    weight_got = send(weight, y=NEAR)

    freq = 10000.0 ** (-(2.0 * jnp.arange(HALF, dtype=F32)) / HD)
    angle = freq[:, None] * positions.astype(F32)[None, :]
    cos, sin = jnp.cos(angle), jnp.sin(angle)
    back, cos, sin = back_of(key_cotangent, cos, sin)

    weight = jnp.concatenate([weight, weight_got])
    back, weight = tie((back, weight))
    weight_got = send(weight, y=BACK)

    far, far_sib = grad_half(at, back, tokens, 1)
    far_got = send(far_sib, core=(1, 1))
    weight = jnp.concatenate([weight, weight_got])
    far, back, weight = tie((far, back, weight))
    weight_got = send(weight[:2], z=NEAR)
    near, near_sib = grad_half(at, back, tokens, 0)
    near, near_sib, far_got, weight_got = tie((near, near_sib, far_got, weight_got))
    near_got = send(near_sib, core=(1, 1))
    weight_more = send(weight[2:], z=NEAR)

    def total(own, got, ax, ay):
        return own[:, ax, :, ay] + got[:, ax, :, ay].astype(F32)

    both = slice(None)
    far_in = send(total(far, far_got, 1, both).astype(BF16), x=NEAR)
    near_in = send(total(near, near_got, both, 1).astype(BF16), y=NEAR)
    weight = jnp.concatenate([weight, weight_got, weight_more])
    weight_got = send(weight, z=BACK)
    far_sent = (total(far, far_got, 0, 1) + far_in[:, :, 1].astype(F32)).astype(BF16)
    near_sent = (total(near, near_got, 1, 0) + near_in[:, 1].astype(F32)).astype(BF16)
    far = total(far, far_got, 0, both) + far_in.astype(F32)
    near = total(near, near_got, both, 0) + near_in.astype(F32)
    far_in = send(far_sent, y=NEAR)
    near_in = send(near_sent, x=NEAR)
    mine = sums(at, near, near_in, far, far_in).reshape(16, 64, 512)
    got = lax.all_to_all(mine, BITS, 0, 0, axis_index_groups=quads(), tiled=True)
    at, weight_got, _ = tie((at, weight_got, mine))
    weight = jnp.concatenate([weight, weight_got])
    weight_sib = send(weight, core=(1, 1))
    half = forward(at, tokens, weight)
    keys = forward(at, tokens, weight_sib, half, cos, sin)
    keys, got = tie((keys, got))
    return keys, jnp.sum(got.astype(F32), axis=0)


def solution(mesh):
    bits = Mesh(mesh.devices.reshape((2,) * 7), BITS)
    tokens, weight = P(BITS, None), P(("yhi", "ylo", "zhi", "core"), None)
    return jax.shard_map(
        local,
        mesh=bits,
        in_specs=(tokens, P(BITS), weight, weight, tokens),
        out_specs=(tokens, tokens),
        check_vma=False,
    )
```

time: 334 us -> 98.6 us (0.30)
  waiting for transfers between devices: 213 us -> 25.6 us
  matrix products: 38.3 us -> 0 us
  Pallas kernels: 0 us -> 36.9 us
  local copies, waits for them, and re-layouts: 39.8 us -> 7.04 us
  blocking collectives: 25.5 us -> 0 us
  starting transfers between devices: 0.12 us -> 22.4 us
  between operations: 13.8 us -> 0.88 us
    reduce_scatter x2 -> x0, waiting for transfers between devices: 183 us -> none  [the longest x1 145 us: local(): within = lax.psum_scatter(shaped, 'local', scatter_dimension=1, tiled=True)]
    dot_general x2 -> x0, matrix products: 38.3 us -> none  [the longest x1 22.6 us: local(): raw = jnp.dot(tokens, weight, preferred_element_type=jnp.float32)]
    pallas_call x0 -> x7, Pallas kernels: none -> 36.9 us  [the longest x2 18.4 us: forward(): pl.pallas_call(lambda *refs: forward_kernel(int(bool(rest)), *refs), in_s...]
    all_gather x1 -> x0, waiting for transfers between devices: 28.8 us -> none  [local(): codes = lax.all_gather(weight_codes, 'local', axis=0, tiled=True)]
    ppermute x0 -> x12, waiting for transfers between devices: none -> 25.6 us  [send(): return lax.ppermute(value, BITS, pairs)]
    all_gather x1 -> x0, blocking collectives: 25.5 us -> none  [local(): lax.all_gather(weight_scales.astype(jnp.bfloat16), 'local', axis=0, tiled...]
    reshape x2 -> x0, local copies, waits for them, and re-layouts: 18 us -> none  [the longest x1 17.4 us: local(): shaped = partial_grad.reshape(n_node, depth // n_node, width)]
    ppermute x0 -> x12, starting transfers between devices: none -> 15.1 us  [send(): return lax.ppermute(value, BITS, pairs)]
  transfers between devices with their start and end apart: 3 -> 13, of which waited for: 3 -> 8; matrix products, arithmetic and copies ran while one was open for 7% -> 8% of each run, Pallas kernels for 0% -> 37%
where the time goes in v1:
time: 98.6 us; the launch traced here: 98 us
  Pallas kernels  36.9 us (37%)
  waiting for transfers between devices  25.6 us (26%)
  starting transfers between devices  22.4 us (23%)
  local copies, waits for them, and re-layouts  7.04 us (7%)
  other arithmetic  5.13 us (5%)
    ppermute x12, waiting for transfers between devices, send(): return lax.ppermute(value, BITS, pairs)  25.6 us
    pallas_call x2, Pallas kernels, forward(): pl.pallas_call(lambda *refs: forward_kernel(int(bool(rest)), *refs), in_s...  18.4 us
    ppermute x12, starting transfers between devices, send(): return lax.ppermute(value, BITS, pairs)  15.1 us
    pallas_call x2, Pallas kernels, grad_half(): pl.pallas_call(lambda *refs: grad_kernel(chunk, *refs), in_specs=[SCALAR,...  14.9 us
    all_to_all x1, starting transfers between devices, local(): lax.all_to_all(mine, BITS, 0, 0, axis_index_groups=quads(), tiled=True)  7.38 us
    unnamed x9, local copies, waits for them, and re-layouts  4.56 us
  transfers between devices with their start and end apart: 13, of which 8 were waited for; matrix products, arithmetic and copies ran while one was open for 8% of the time, Pallas kernels for 37%

profile of v1, /device:TPU:0, one launch (start us, length us, event | category | flops | bytes accessed | tf_op | source)
XLA Modules:
  0.0 98.0 jit_solution(3428380060787351539)
XLA Ops:
  0.7 1.1 %copy-done.1 = bf16[512,512]{1,0:T(8,128)(2,1)S(1)} copy-done((bf16[512,512]{1,0:T(8,128)(2,1)S(1)}, bf16[512,512]{1,0:T(8,128)(2,1)}, u32[]{:S(2)}) %copy-start.1) | copy-done | bytes 524312
  1.9 0.7 copy-done.2
  2.5 0.9 weight.1
  3.4 1.7 %collective-permute-start = (bf16[1,256,512]{2,1,0:T(8,128)(2,1)S(1)}, bf16[1,256,512]{2,1,0:T(8,128)(2,1)S(1)}, u32[]{:S(2)}, u32[]{:S(2)}) collective-permute-start(bf16[1,256,512]{2,1,0:T(8,128)(2,1)S(1)} %weight.1), channel_id=1, source_target_pairs={{0,4},{1,13},{2,6},{3,15},{4,0},{5,9},{6,2},{7,11},{8,12},{9,5},{1... | collective-permute-start | bytes 786440 | tf_op jit(solution)/shard_map/ppermute | solution.py:50
  5.2 0.7 convert_element_type.66
  5.9 1.0 %multiply_sine_fusion = (f32[64,1024]{1,0:T(8,128)S(1)}, f32[64,1024]{1,0:T(8,128)S(1)}) fusion(f32[1024]{0:T(1024)S(1)} %convert_element_type.66, f32[64]{0:T(128)S(1)} %multiply_power_fusion), kind=kLoop, calls=%fused_computation.26 | loop fusion | flops 65536 | bytes 528640 | tf_op jit(solution)/shard_map/sin | solution.py:239
  6.9 0.9 back.1
  7.8 2.1 %collective-permute-done = bf16[1,256,512]{2,1,0:T(8,128)(2,1)S(1)} collective-permute-done((bf16[1,256,512]{2,1,0:T(8,128)(2,1)S(1)}, bf16[1,256,512]{2,1,0:T(8,128)(2,1)S(1)}, u32[]{:S(2)}, u32[]{:S(2)}) %collective-permute-start) | collective-permute-done | bytes 262176 | tf_op jit(solution)/shard_map/ppermute | solution.py:50
  9.9 3.2 %collective-permute-start.1 = (bf16[2,256,512]{2,1,0:T(8,128)(2,1)S(1)}, bf16[2,256,512]{2,1,0:T(8,128)(2,1)S(1)}, u32[]{:S(2)}, u32[]{:S(2)}) collective-permute-start(bf16[2,256,512]{2,1,0:T(8,128)(2,1)S(1)} %pad_maximum_fusion.2), channel_id=1, source_target_pairs={{0,12},{1,5},{2,14},{3,7},{4,8},{5,1},{6,10},{7,3},{8,4},{9,13},{1... | collective-permute-start | bytes 1572872 | tf_op jit(solution)/shard_map/ppermute | solution.py:50
  13.1 7.5 %grad.2 = (f32[2,2,2,2,2,64,512]{6,5,4,3,2,1,0:T(8,128)S(1)}, bf16[2,2,2,2,2,64,512]{6,5,4,3,2,1,0:T(8,128)(2,1)S(1)}) custom-call(s32[5]{0:T(128)S(1)} %stack.23.at.refs_0_, bf16[1024,512]{1,0:T(8,128)(2,1)S(1)} %get-tuple-element.27.refs_1_, bf16[1024,8192]{1,0:T(8,128)(2,1)} %refs_1_.3), custom_call_target="tpu_custom_call" | custom-call | flops 42949672960 | bytes 8388608 | tf_op jit(solution)/shard_map/grad/pallas_call | solution.py:133
  21.1 2.0 %collective-permute-start.3 = (bf16[2,256,512]{2,1,0:T(8,128)(2,1)S(1)}, bf16[2,256,512]{2,1,0:T(8,128)(2,1)S(1)}, u32[]{:S(2)}, u32[]{:S(2)}) collective-permute-start(bf16[2,256,512]{2,1,0:T(8,128)(2,1)S(1)} %get-tuple-element.42), channel_id=1, source_target_pairs={{0,64},{1,67},{2,66},{3,65},{4,68},{5,71},{6,70},{7,69},{8,72},{9,... | collective-permute-start | bytes 1572872 | tf_op jit(solution)/shard_map/ppermute | solution.py:50
  23.1 7.4 %grad.3 = (f32[2,2,2,2,2,64,512]{6,5,4,3,2,1,0:T(8,128)S(1)}, bf16[2,2,2,2,2,64,512]{6,5,4,3,2,1,0:T(8,128)(2,1)S(1)}) custom-call(s32[5]{0:T(128)S(1)} %stack.23.at.refs_0_, bf16[1024,512]{1,0:T(8,128)(2,1)S(1)} %get-tuple-element.27.refs_1_, bf16[1024,8192]{1,0:T(8,128)(2,1)} %refs_1_.3), custom_call_target="tpu_custom_call" | custom-call | flops 42949672960 | bytes 8388608 | tf_op jit(solution)/shard_map/grad/pallas_call | solution.py:133
  30.7 2.4 %collective-permute-start.6 = (bf16[2,2,2,2,2,64,512]{6,5,4,2,0,1,3:T(8,128)(2,1)S(1)}, bf16[2,2,2,2,2,64,512]{6,5,4,2,0,1,3:T(8,128)(2,1)S(1)}, u32[]{:S(2)}, u32[]{:S(2)}) collective-permute-start(bf16[2,2,2,2,2,64,512]{6,5,4,2,0,1,3:T(8,128)(2,1)S(1)} %copy.9), channel_id=1, source_target_pairs={{0,1},{1,0},{2,3},{3,2},{4,5},{5,4},{6,7},{7,6},{8,9},{9,8},{10,11... | collective-permute-start | bytes 6291464 | tf_op jit(solution)/shard_map/ppermute | solution.py:50
  33.5 1.6 %collective-permute-start.9 = (bf16[2,2,2,2,64,512]{5,4,3,1,0,2:T(8,128)(2,1)S(1)}, bf16[2,2,2,2,64,512]{5,4,3,1,0,2:T(8,128)(2,1)S(1)}, u32[]{:S(2)}, u32[]{:S(2)}) collective-permute-start(bf16[2,2,2,2,64,512]{5,4,3,1,0,2:T(8,128)(2,1)S(1)} %fusion.7), channel_id=1, source_target_pairs={{0,16},{1,49},{2,18},{3,51},{4,20},{5,53},{6,22},{7,55},{8,24},{9,... | collective-permute-start | bytes 3145736 | tf_op jit(solution)/shard_map/ppermute | solution.py:50
  35.1 1.8 %collective-permute-done.6 = bf16[2,2,2,2,2,64,512]{6,5,4,2,0,1,3:T(8,128)(2,1)S(1)} collective-permute-done((bf16[2,2,2,2,2,64,512]{6,5,4,2,0,1,3:T(8,128)(2,1)S(1)}, bf16[2,2,2,2,2,64,512]{6,5,4,2,0,1,3:T(8,128)(2,1)S(1)}, u32[]{:S(2)}, u32[]{:S(2)}) %collective-permute-start.6) | collective-permute-done | bytes 2097184 | tf_op jit(solution)/shard_map/ppermute | solution.py:50
  37.5 4.7 %collective-permute-done.4 = bf16[2,256,512]{2,1,0:T(8,128)(2,1)S(1)} collective-permute-done((bf16[2,256,512]{2,1,0:T(8,128)(2,1)S(1)}, bf16[2,256,512]{2,1,0:T(8,128)(2,1)S(1)}, u32[]{:S(2)}, u32[]{:S(2)}) %collective-permute-start.4) | collective-permute-done | bytes 524320 | tf_op jit(solution)/shard_map/ppermute | solution.py:50
  42.5 2.1 %collective-permute-start.5 = (bf16[8,256,512]{2,1,0:T(8,128)(2,1)S(1)}, bf16[8,256,512]{2,1,0:T(8,128)(2,1)S(1)}, u32[]{:S(2)}, u32[]{:S(2)}) collective-permute-start(bf16[8,256,512]{2,1,0:T(8,128)(2,1)S(1)} %pad_maximum_fusion), channel_id=1, source_target_pairs={{0,66},{1,65},{2,64},{3,67},{4,70},{5,69},{6,68},{7,71},{8,74},{9,... | collective-permute-start | bytes 6291464 | tf_op jit(solution)/shard_map/ppermute | solution.py:50
  44.7 1.0 %constant_dynamic-update-slice_fusion.3 = bf16[16,256,512]{2,1,0:T(8,128)(2,1)} fusion(bf16[4,256,512]{2,1,0:T(8,128)(2,1)S(1)} %pad_maximum_fusion.1), kind=kLoop, calls=%fused_computation.31 | loop fusion | bytes 2097152
  45.7 0.8 constant_dynamic-update-slice_fusion.2
  46.5 0.9 constant_dynamic-update-slice_fusion.1
  47.4 1.0 collective-permute-done.9
  48.8 3.4 %collective-permute-done.7 = bf16[2,2,2,2,64,512]{5,4,3,2,0,1:T(8,128)(2,1)S(1)} collective-permute-done((bf16[2,2,2,2,64,512]{5,4,3,2,0,1:T(8,128)(2,1)S(1)}, bf16[2,2,2,2,64,512]{5,4,3,2,0,1:T(8,128)(2,1)S(1)}, u32[]{:S(2)}, u32[]{:S(2)}) %collective-permute-start.7) | collective-permute-done | bytes 1048608 | tf_op jit(solution)/shard_map/ppermute | solution.py:50
  52.5 1.6 %collective-permute-start.8 = (bf16[2,2,2,64,512]{4,3,2,1,0:T(8,128)(2,1)S(1)}, bf16[2,2,2,64,512]{4,3,2,1,0:T(8,128)(2,1)S(1)}, u32[]{:S(2)}, u32[]{:S(2)}) collective-permute-start(bf16[2,2,2,64,512]{4,3,2,1,0:T(8,128)(2,1)S(1)} %fusion.13), channel_id=1, source_target_pairs={{0,16},{1,49},{2,18},{3,51},{4,20},{5,53},{6,22},{7,55},{8,24},{9,... | collective-permute-start | bytes 1572872 | tf_op jit(solution)/shard_map/ppermute | solution.py:50
  55.5 2.4 %collective-permute-done.10.far_in_ref = bf16[2,2,2,64,512]{4,3,2,1,0:T(8,128)(2,1)S(1)} collective-permute-done((bf16[2,2,2,64,512]{4,3,2,1,0:T(8,128)(2,1)S(1)}, bf16[2,2,2,64,512]{4,3,2,1,0:T(8,128)(2,1)S(1)}, u32[]{:S(2)}, u32[]{:S(2)}) %collective-permute-start.10) | collective-permute-done | bytes 524320 | tf_op jit(solution)/shard_map/ppermute | solution.py:50
  57.9 3.9 %collective-permute-done.8.near_in_ref = bf16[2,2,2,64,512]{4,3,2,1,0:T(8,128)(2,1)S(1)} collective-permute-done((bf16[2,2,2,64,512]{4,3,2,1,0:T(8,128)(2,1)S(1)}, bf16[2,2,2,64,512]{4,3,2,1,0:T(8,128)(2,1)S(1)}, u32[]{:S(2)}, u32[]{:S(2)}) %collective-permute-start.8) | collective-permute-done | bytes 524320 | tf_op jit(solution)/shard_map/ppermute | solution.py:50
  61.7 1.8 %sums.1 = bf16[2,2,2,2,64,512]{5,4,3,2,1,0:T(8,128)(2,1)} custom-call(s32[5]{0:T(128)S(1)} %stack.23.at.refs_0_, f32[2,2,2,2,64,512]{5,4,3,2,1,0:T(8,128)S(1)} %copy.15.near_ref, bf16[2,2,2,64,512]{4,3,2,1,0:T(8,128)(2,1)S(1)} %collective-permute-done.8.near_in_ref, f32[2,2,2,2,64,512]{5,4,3,2,1,0:T(8,128)S(1)} %copy.16.far_ref, ...), custom_call_target="tpu_custom_call" | custom-call | tf_op jit(solution)/shard_map/sums/pallas_call | solution.py:219
  63.5 6.3 %collective-permute-done.5 = bf16[8,256,512]{2,1,0:T(8,128)(2,1)S(1)} collective-permute-done((bf16[8,256,512]{2,1,0:T(8,128)(2,1)S(1)}, bf16[8,256,512]{2,1,0:T(8,128)(2,1)S(1)}, u32[]{:S(2)}, u32[]{:S(2)}) %collective-permute-start.5) | collective-permute-done | bytes 2097184 | tf_op jit(solution)/shard_map/ppermute | solution.py:50
  69.9 1.5 %constant_dynamic-update-slice_fusion.refs_2_ = bf16[16,256,512]{2,1,0:T(8,128)(2,1)} fusion(bf16[16,256,512]{2,1,0:T(8,128)(2,1)} %constant_dynamic-update-slice_fusion.1, bf16[8,256,512]{2,1,0:T(8,128)(2,1)S(1)} %collective-permute-done.5), kind=kLoop, calls=%fused_computation.28 | loop fusion | bytes 4194304 | tf_op jit(solution)/shard_map/concatenate | solution.py:273
  71.4 7.4 %all-to-all-start = ((bf16[16,64,512]{2,1,0:T(8,128)(2,1)}), bf16[16,64,512]{2,1,0:T(8,128)(2,1)S(1)}, u32[]{:S(2)}, u32[]{:S(2)}) async-start(bf16[16,64,512]{2,1,0:T(8,128)(2,1)} %bitcast.14), calls=%async_computation | async-start | bytes 2097152 | tf_op jit(solution)/shard_map/all_to_all | solution.py:271
  78.8 8.3 %forward.2.refs_3_ = f32[1024,512]{1,0:T(8,128)S(1)} custom-call(s32[5]{0:T(128)S(1)} %stack.23.at.refs_0_, bf16[1024,8192]{1,0:T(8,128)(2,1)} %refs_1_.3, bf16[16,256,512]{2,1,0:T(8,128)(2,1)} %constant_dynamic-update-slice_fusion.refs_2_), custom_call_target="tpu_custom_call" | custom-call | flops 17179869184 | bytes 4194304 | tf_op jit(solution)/shard_map/forward/pallas_call | solution.py:191
  87.2 10.0 %forward.3 = bf16[1024,512]{1,0:T(8,128)(2,1)} custom-call(s32[5]{0:T(128)S(1)} %stack.23.at.refs_0_, bf16[1024,8192]{1,0:T(8,128)(2,1)} %refs_1_.3, bf16[16,256,512]{2,1,0:T(8,128)(2,1)} %collective-permute-done.11.refs_2_, f32[1024,512]{1,0:T(8,128)S(1)} %forward.2.refs_3_, f32[1024,128]{1,0:T(8,128)S(1)} %get-tuple-element.38.refs_4_, ...), custom_call_target="tpu_custom_call" | custom-call | flops 17179869184 | bytes 4194304 | tf_op jit(solution)/shard_map/forward/pallas_call | solution.py:191
  97.2 0.8 convert_reduce_fusion
  (30 shorter events, 4.1 us)
Async XLA Ops:
  0.6 6.2 %copy-start = (bf16[1024,512]{1,0:T(8,128)(2,1)S(1)}, bf16[1024,512]{1,0:T(8,128)(2,1)}, u32[]{:S(2)}) copy-start(bf16[1024,512]{1,0:T(8,128)(2,1)} %cotangent_ref.1) | copy-start | bytes 3145732
  0.7 1.1 %copy-start.1 = (bf16[512,512]{1,0:T(8,128)(2,1)S(1)}, bf16[512,512]{1,0:T(8,128)(2,1)}, u32[]{:S(2)}) copy-start(bf16[512,512]{1,0:T(8,128)(2,1)} %codes_ref.1) | copy-start | bytes 1572868
  1.9 0.7 copy-start.2
  3.4 6.5 %collective-permute-start = (bf16[1,256,512]{2,1,0:T(8,128)(2,1)S(1)}, bf16[1,256,512]{2,1,0:T(8,128)(2,1)S(1)}, u32[]{:S(2)}, u32[]{:S(2)}) collective-permute-start(bf16[1,256,512]{2,1,0:T(8,128)(2,1)S(1)} %weight.1), channel_id=1, source_target_pairs={{0,4},{1,13},{2,6},{3,15},{4,0},{5,9},{6,2},{7,11},{8,12},{9,5},{1... | collective-permute-start | bytes 786440 | tf_op jit(solution)/shard_map/ppermute | solution.py:50
  9.9 11.0 %collective-permute-start.1 = (bf16[2,256,512]{2,1,0:T(8,128)(2,1)S(1)}, bf16[2,256,512]{2,1,0:T(8,128)(2,1)S(1)}, u32[]{:S(2)}, u32[]{:S(2)}) collective-permute-start(bf16[2,256,512]{2,1,0:T(8,128)(2,1)S(1)} %pad_maximum_fusion.2), channel_id=1, source_target_pairs={{0,12},{1,5},{2,14},{3,7},{4,8},{5,1},{6,10},{7,3},{8,4},{9,13},{1... | collective-permute-start | bytes 1572872 | tf_op jit(solution)/shard_map/ppermute | solution.py:50
  20.8 9.7 %collective-permute-start.2 = (bf16[2,2,2,2,2,64,512]{6,5,4,2,0,3,1:T(8,128)(2,1)S(1)}, bf16[2,2,2,2,2,64,512]{6,5,4,2,0,3,1:T(8,128)(2,1)S(1)}, u32[]{:S(2)}, u32[]{:S(2)}) collective-permute-start(bf16[2,2,2,2,2,64,512]{6,5,4,2,0,3,1:T(8,128)(2,1)S(1)} %copy.7), channel_id=1, source_target_pairs={{0,1},{1,0},{2,3},{3,2},{4,5},{5,4},{6,7},{7,6},{8,9},{9,8},{10,11... | collective-permute-start | bytes 6291464 | tf_op jit(solution)/shard_map/ppermute | solution.py:50
  21.1 9.5 %collective-permute-start.3 = (bf16[2,256,512]{2,1,0:T(8,128)(2,1)S(1)}, bf16[2,256,512]{2,1,0:T(8,128)(2,1)S(1)}, u32[]{:S(2)}, u32[]{:S(2)}) collective-permute-start(bf16[2,256,512]{2,1,0:T(8,128)(2,1)S(1)} %get-tuple-element.42), channel_id=1, source_target_pairs={{0,64},{1,67},{2,66},{3,65},{4,68},{5,71},{6,70},{7,69},{8,72},{9,... | collective-permute-start | bytes 1572872 | tf_op jit(solution)/shard_map/ppermute | solution.py:50
  30.7 6.2 %collective-permute-start.6 = (bf16[2,2,2,2,2,64,512]{6,5,4,2,0,1,3:T(8,128)(2,1)S(1)}, bf16[2,2,2,2,2,64,512]{6,5,4,2,0,1,3:T(8,128)(2,1)S(1)}, u32[]{:S(2)}, u32[]{:S(2)}) collective-permute-start(bf16[2,2,2,2,2,64,512]{6,5,4,2,0,1,3:T(8,128)(2,1)S(1)} %copy.9), channel_id=1, source_target_pairs={{0,1},{1,0},{2,3},{3,2},{4,5},{5,4},{6,7},{7,6},{8,9},{9,8},{10,11... | collective-permute-start | bytes 6291464 | tf_op jit(solution)/shard_map/ppermute | solution.py:50
  33.1 9.2 %collective-permute-start.4 = (bf16[2,256,512]{2,1,0:T(8,128)(2,1)S(1)}, bf16[2,256,512]{2,1,0:T(8,128)(2,1)S(1)}, u32[]{:S(2)}, u32[]{:S(2)}) collective-permute-start(bf16[2,256,512]{2,1,0:T(8,128)(2,1)S(1)} %get-tuple-element.43), channel_id=1, source_target_pairs={{0,64},{1,67},{2,66},{3,65},{4,68},{5,71},{6,70},{7,69},{8,72},{9,... | collective-permute-start | bytes 1572872 | tf_op jit(solution)/shard_map/ppermute | solution.py:50
  33.5 14.9 %collective-permute-start.9 = (bf16[2,2,2,2,64,512]{5,4,3,1,0,2:T(8,128)(2,1)S(1)}, bf16[2,2,2,2,64,512]{5,4,3,1,0,2:T(8,128)(2,1)S(1)}, u32[]{:S(2)}, u32[]{:S(2)}) collective-permute-start(bf16[2,2,2,2,64,512]{5,4,3,1,0,2:T(8,128)(2,1)S(1)} %fusion.7), channel_id=1, source_target_pairs={{0,16},{1,49},{2,18},{3,51},{4,20},{5,53},{6,22},{7,55},{8,24},{9,... | collective-permute-start | bytes 3145736 | tf_op jit(solution)/shard_map/ppermute | solution.py:50
  37.3 14.9 %collective-permute-start.7 = (bf16[2,2,2,2,64,512]{5,4,3,2,0,1:T(8,128)(2,1)S(1)}, bf16[2,2,2,2,64,512]{5,4,3,2,0,1:T(8,128)(2,1)S(1)}, u32[]{:S(2)}, u32[]{:S(2)}) collective-permute-start(bf16[2,2,2,2,64,512]{5,4,3,2,0,1:T(8,128)(2,1)S(1)} %fusion.6), channel_id=1, source_target_pairs={{0,4},{1,13},{2,6},{3,15},{4,0},{5,9},{6,2},{7,11},{8,12},{9,5},{1... | collective-permute-start | bytes 3145736 | tf_op jit(solution)/shard_map/ppermute | solution.py:50
  42.5 27.3 %collective-permute-start.5 = (bf16[8,256,512]{2,1,0:T(8,128)(2,1)S(1)}, bf16[8,256,512]{2,1,0:T(8,128)(2,1)S(1)}, u32[]{:S(2)}, u32[]{:S(2)}) collective-permute-start(bf16[8,256,512]{2,1,0:T(8,128)(2,1)S(1)} %pad_maximum_fusion), channel_id=1, source_target_pairs={{0,66},{1,65},{2,64},{3,67},{4,70},{5,69},{6,68},{7,71},{8,74},{9,... | collective-permute-start | bytes 6291464 | tf_op jit(solution)/shard_map/ppermute | solution.py:50
  48.6 9.3 %collective-permute-start.10 = (bf16[2,2,2,64,512]{4,3,2,1,0:T(8,128)(2,1)S(1)}, bf16[2,2,2,64,512]{4,3,2,1,0:T(8,128)(2,1)S(1)}, u32[]{:S(2)}, u32[]{:S(2)}) collective-permute-start(bf16[2,2,2,64,512]{4,3,2,1,0:T(8,128)(2,1)S(1)} %fusion.10), channel_id=1, source_target_pairs={{0,4},{1,13},{2,6},{3,15},{4,0},{5,9},{6,2},{7,11},{8,12},{9,5},{1... | collective-permute-start | bytes 1572872 | tf_op jit(solution)/shard_map/ppermute | solution.py:50
  52.5 9.3 %collective-permute-start.8 = (bf16[2,2,2,64,512]{4,3,2,1,0:T(8,128)(2,1)S(1)}, bf16[2,2,2,64,512]{4,3,2,1,0:T(8,128)(2,1)S(1)}, u32[]{:S(2)}, u32[]{:S(2)}) collective-permute-start(bf16[2,2,2,64,512]{4,3,2,1,0:T(8,128)(2,1)S(1)} %fusion.13), channel_id=1, source_target_pairs={{0,16},{1,49},{2,18},{3,51},{4,20},{5,53},{6,22},{7,55},{8,24},{9,... | collective-permute-start | bytes 1572872 | tf_op jit(solution)/shard_map/ppermute | solution.py:50
  71.4 15.7 %collective-permute-start.11 = (bf16[16,256,512]{2,1,0:T(8,128)(2,1)}, bf16[16,256,512]{2,1,0:T(8,128)(2,1)}, u32[]{:S(2)}, u32[]{:S(2)}) collective-permute-start(bf16[16,256,512]{2,1,0:T(8,128)(2,1)} %constant_dynamic-update-slice_fusion.refs_2_), channel_id=1, source_target_pairs={{0,1},{1,0},{2,3},{3,2},{4,5},{5,4},{6,7},{7,6},{8,9},{9,8},{10,11... | collective-permute-start | bytes 12582920 | tf_op jit(solution)/shard_map/ppermute | solution.py:50
  71.4 25.8 %all-to-all-start = ((bf16[16,64,512]{2,1,0:T(8,128)(2,1)}), bf16[16,64,512]{2,1,0:T(8,128)(2,1)S(1)}, u32[]{:S(2)}, u32[]{:S(2)}) async-start(bf16[16,64,512]{2,1,0:T(8,128)(2,1)} %bitcast.14), calls=%async_computation | async-start | bytes 2097152 | tf_op jit(solution)/shard_map/all_to_all | solution.py:271

commit v2 on v1

--- a/solution.py
+++ b/solution.py
@@ -14,6 +14,7 @@
 BITS = ("zlo", "xhi", "xlo", "yhi", "ylo", "zhi", "core")
 LIMIT = 8 * MIB
 LARGE = 36 * MIB
+COVER = 4
 VMEM = pl.BlockSpec(memory_space=pltpu.VMEM)
 SCALAR = pl.BlockSpec(memory_space=pltpu.SMEM)
 NEAR, BACK = (1, 3), (3, 1)
@@ -40,14 +41,15 @@
 STAY = (0, 0)
 
 
-def send(value, x=STAY, y=STAY, z=STAY, core=STAY):
+def send(what, value, x=STAY, y=STAY, z=STAY, core=STAY):
     pairs = []
     for src in range(128):
         at_x, at_y, zlo, zhi, at_core = coordinates(src)
         at_z = (2 * zhi + zlo) ^ z[at_core]
         place = ((at_z & 1) << 6) | ((at_x ^ x[at_core]) << 4) | ((at_y ^ y[at_core]) << 2) | ((at_z >> 1) << 1)
         pairs.append((src, place | (at_core ^ core[at_core])))
-    return lax.ppermute(value, BITS, pairs)
+    with jax.named_scope(what):
+        return lax.ppermute(value, BITS, pairs)
 
 
 def held_at(distance, core):
@@ -76,24 +78,24 @@
     )(at, codes, scales)
 
 
-def back_kernel(cotangent_ref, cos_ref, sin_ref, back_ref, cos2_ref, sin2_ref):
-    cos = jnp.concatenate([cos_ref[...], cos_ref[...]], axis=0).T
-    sin = jnp.concatenate([-sin_ref[...], sin_ref[...]], axis=0).T
-    cos2_ref[...] = cos
-    sin2_ref[...] = sin
+def head_turn(cos_ref, sin_ref):
+    cos, sin = cos_ref[...], sin_ref[...]
+    return jnp.concatenate([cos, cos], axis=0).T, jnp.concatenate([-sin, sin], axis=0).T
+
+
+def back_kernel(cotangent_ref, cos_ref, sin_ref, back_ref):
+    cos, sin = head_turn(cos_ref, sin_ref)
     for head in range(4):
         given = cotangent_ref[:, head * HD : (head + 1) * HD].astype(F32)
         back_ref[:, head * HD : (head + 1) * HD] = (given * cos - pltpu.roll(given, HALF, 1) * sin).astype(BF16)
 
 
 def back_of(cotangent, cos, sin):
-    rows, width = cotangent.shape
-    turn = jax.ShapeDtypeStruct((rows, HD), F32)
     return pl.pallas_call(
         back_kernel,
         in_specs=[VMEM] * 3,
-        out_specs=[VMEM] * 3,
-        out_shape=[jax.ShapeDtypeStruct((rows, width), BF16), turn, turn],
+        out_specs=VMEM,
+        out_shape=jax.ShapeDtypeStruct(cotangent.shape, BF16),
         compiler_params=pltpu.CompilerParams(vmem_limit_bytes=LIMIT),
         name="back",
     )(cotangent, cos, sin)
@@ -145,8 +147,9 @@
     )(at, back, tokens)
 
 
-def forward_kernel(other, at, tokens_ref, weight_ref, *rest):
+def forward_kernel(other, at, tokens_ref, *rest):
     y, zlo, zhi, core = at[1], at[2], at[3], at[4]
+    parts, rest = rest[:4], rest[4:]
     acc, weight, block, arrived, filled = rest[-5:]
     holder = core ^ other
 
@@ -154,43 +157,49 @@
         column = pl.multiple_of((2 * i + holder) * 512, 512)
         return pltpu.make_async_copy(tokens_ref.at[:, pl.ds(column, 512)], block.at[i], arrived.at[i])
 
-    def fill(i, to_zlo):
+    def fill(i, to_zlo, ref, place):
+        rows = pl.ds(to_zlo * 256, 256)
+        return pltpu.make_async_copy(ref.at[place], weight.at[i, rows], filled.at[2 * i + to_zlo])
+
+    def start_fill(i, to_zlo):
         from_y = held_at(y ^ (i // 2), holder)
         from_z = held_at((2 * zhi + zlo) ^ (2 * (i % 2) + to_zlo), holder)
-        rows = pl.ds(to_zlo * 256, 256)
-        return pltpu.make_async_copy(
-            weight_ref.at[from_z * 4 + from_y], weight.at[i, rows], filled.at[2 * i + to_zlo]
-        )
+        for n, ref in enumerate(parts):
+
+            @pl.when((from_z // 2) * 2 + from_y // 2 == n)
+            def _():
+                fill(i, to_zlo, ref, (from_z % 2) * 2 + from_y % 2).start()
 
     for i in range(8):
         fetch(i).start()
-        fill(i, 0).start()
-        fill(i, 1).start()
+        start_fill(i, 0)
+        start_fill(i, 1)
     acc[...] = rest[0][...] if other else jnp.zeros_like(acc)
 
     @pl.loop(0, 8)
     def _(i):
         fetch(i).wait()
-        fill(i, 0).wait()
-        fill(i, 1).wait()
+        fill(i, 0, parts[0], 0).wait()
+        fill(i, 1, parts[0], 0).wait()
         acc[...] += jnp.dot(block[i], weight[i], preferred_element_type=F32)
 
     if other:
-        cos_ref, sin_ref, keys_ref = rest[1:4]
+        cos, sin = head_turn(*rest[1:3])
+        keys_ref = rest[3]
         for head in range(4):
             raw = acc[:, head * HD : (head + 1) * HD]
             turned = pltpu.roll(raw, HALF, 1)
-            keys_ref[:, head * HD : (head + 1) * HD] = (raw * cos_ref[...] + turned * sin_ref[...]).astype(BF16)
-
-
-def forward(at, tokens, weight, *rest):
+            keys_ref[:, head * HD : (head + 1) * HD] = (raw * cos + turned * sin).astype(BF16)
+
+
+def forward(at, tokens, parts, *rest):
     rows, depth = tokens.shape
-    width = weight.shape[-1]
+    width = parts[0].shape[-1]
     hbm = pl.BlockSpec(memory_space=pltpu.HBM)
     total = pltpu.VMEM((rows, width), F32)
     return pl.pallas_call(
         lambda *refs: forward_kernel(int(bool(rest)), *refs),
-        in_specs=[SCALAR, hbm, hbm] + [VMEM] * len(rest),
+        in_specs=[SCALAR] + [hbm] * 5 + [VMEM] * len(rest),
         out_specs=VMEM,
         scratch_shapes=[total] * bool(rest)
         + [
@@ -201,9 +210,34 @@
         ],
         out_shape=jax.ShapeDtypeStruct((rows, width), BF16 if rest else F32),
         compiler_params=pltpu.CompilerParams(vmem_limit_bytes=LARGE),
-        cost_estimate=pl.CostEstimate(flops=4 * rows * depth * width, bytes_accessed=4 * MIB, transcendentals=0),
+        cost_estimate=pl.CostEstimate(flops=COVER * rows * depth * width, bytes_accessed=4 * MIB, transcendentals=0),
         name="forward",
-    )(at, tokens, weight, *rest)
+    )(at, tokens, *parts, *rest)
+
+
+def total_kernel(got_ref, out_ref, block, arrived):
+    def fetch(i):
+        return pltpu.make_async_copy(got_ref.at[4 * i : 4 * i + 4], block.at[i], arrived.at[i])
+
+    for i in range(4):
+        fetch(i).start()
+    for i in range(4):
+        fetch(i).wait()
+        part = jnp.sum(block[i].astype(F32), axis=0)
+        out_ref[...] = part if i == 0 else out_ref[...] + part
+
+
+def total_of(got):
+    _, rows, width = got.shape
+    return pl.pallas_call(
+        total_kernel,
+        in_specs=[pl.BlockSpec(memory_space=pltpu.HBM)],
+        out_specs=VMEM,
+        scratch_shapes=[pltpu.VMEM((4, 4, rows, width), BF16), pltpu.SemaphoreType.DMA((4,))],
+        out_shape=jax.ShapeDtypeStruct((rows, width), F32),
+        compiler_params=pltpu.CompilerParams(vmem_limit_bytes=LIMIT),
+        name="total",
+    )(got)
 
 
 def sums_kernel(at, near_ref, near_in_ref, far_ref, far_in_ref, out_ref):
@@ -232,50 +266,52 @@
     tie = lax.optimization_barrier
 
     weight = weight_piece(at, weight_codes, weight_scales.T)
-    weight_got = send(weight, y=NEAR)
+    weight_got = send("weight_y_near", weight, y=NEAR)
 
     freq = 10000.0 ** (-(2.0 * jnp.arange(HALF, dtype=F32)) / HD)
     angle = freq[:, None] * positions.astype(F32)[None, :]
     cos, sin = jnp.cos(angle), jnp.sin(angle)
-    back, cos, sin = back_of(key_cotangent, cos, sin)
-
+    back = back_of(key_cotangent, cos, sin)
+
+    far, far_sib = grad_half(at, back, tokens, 1)
+    far, far_sib, back, weight, weight_got = tie((far, far_sib, back, weight, weight_got))
+    far_got = send("far_core", far_sib, core=(1, 1))
     weight = jnp.concatenate([weight, weight_got])
     back, weight = tie((back, weight))
-    weight_got = send(weight, y=BACK)
-
-    far, far_sib = grad_half(at, back, tokens, 1)
-    far_got = send(far_sib, core=(1, 1))
-    weight = jnp.concatenate([weight, weight_got])
-    far, back, weight = tie((far, back, weight))
-    weight_got = send(weight[:2], z=NEAR)
+    weight_got = send("weight_y_back", weight, y=BACK)
+    part_got = send("weight_z_near", weight, z=NEAR)
     near, near_sib = grad_half(at, back, tokens, 0)
-    near, near_sib, far_got, weight_got = tie((near, near_sib, far_got, weight_got))
-    near_got = send(near_sib, core=(1, 1))
-    weight_more = send(weight[2:], z=NEAR)
+    near, near_sib, far_got, weight_got, part_got = tie((near, near_sib, far_got, weight_got, part_got))
+    near_got = send("near_core", near_sib, core=(1, 1))
+    parts = [jnp.concatenate([weight, part_got])]
+    part_got = send("weight_z_near_late", weight_got, z=NEAR)
+    late = [send("weight_z_back", parts[0], z=BACK)]
+    sib = [send("weight_core_0", parts[0], core=(1, 1))]
 
     def total(own, got, ax, ay):
         return own[:, ax, :, ay] + got[:, ax, :, ay].astype(F32)
 
     both = slice(None)
-    far_in = send(total(far, far_got, 1, both).astype(BF16), x=NEAR)
-    near_in = send(total(near, near_got, both, 1).astype(BF16), y=NEAR)
-    weight = jnp.concatenate([weight, weight_got, weight_more])
-    weight_got = send(weight, z=BACK)
+    far_in = send("far_x", total(far, far_got, 1, both).astype(BF16), x=NEAR)
+    near_in = send("near_y", total(near, near_got, both, 1).astype(BF16), y=NEAR)
     far_sent = (total(far, far_got, 0, 1) + far_in[:, :, 1].astype(F32)).astype(BF16)
     near_sent = (total(near, near_got, 1, 0) + near_in[:, 1].astype(F32)).astype(BF16)
     far = total(far, far_got, 0, both) + far_in.astype(F32)
     near = total(near, near_got, both, 0) + near_in.astype(F32)
-    far_in = send(far_sent, y=NEAR)
-    near_in = send(near_sent, x=NEAR)
+    far_in = send("far_y", far_sent, y=NEAR)
+    near_in = send("near_x", near_sent, x=NEAR)
+    part_got, _, _ = tie((part_got, far_sent, near_sent))
+    parts.append(jnp.concatenate([weight_got, part_got]))
+    late.append(send("weight_z_back_late", parts[1], z=BACK))
+    sib += [send("weight_core_1", parts[1], core=(1, 1)), send("weight_core_2", late[0], core=(1, 1))]
     mine = sums(at, near, near_in, far, far_in).reshape(16, 64, 512)
     got = lax.all_to_all(mine, BITS, 0, 0, axis_index_groups=quads(), tiled=True)
-    at, weight_got, _ = tie((at, weight_got, mine))
-    weight = jnp.concatenate([weight, weight_got])
-    weight_sib = send(weight, core=(1, 1))
-    half = forward(at, tokens, weight)
-    keys = forward(at, tokens, weight_sib, half, cos, sin)
+    at, late[1], _ = tie((at, late[1], mine))
+    sib.append(send("weight_core_3", late[1], core=(1, 1)))
+    half = forward(at, tokens, parts + late)
+    keys = forward(at, tokens, sib, half, cos, sin)
     keys, got = tie((keys, got))
-    return keys, jnp.sum(got.astype(F32), axis=0)
+    return keys, total_of(got)
 
 
 def solution(mesh):

time: 98.6 us -> 90.8 us (0.921); the launches traced: 98 us -> 89.1 us
  waiting for transfers between devices: 25.6 us -> 15.9 us
  starting transfers between devices: 22.4 us -> 26.9 us
  local copies, waits for them, and re-layouts: 7.04 us -> 4.46 us
  other arithmetic: 5.13 us -> 3.91 us
    ppermute x12 -> x16, waiting for transfers between devices: 25.6 us -> 15.9 us  [send(): return lax.ppermute(value, BITS, pairs)]
    ppermute x12 -> x16, starting transfers between devices: 15.1 us -> 20 us  [send(): return lax.ppermute(value, BITS, pairs)]
    unnamed x9 -> x8, local copies, waits for them, and re-layouts: 4.56 us -> 2.66 us
  transfers between devices with their start and end apart: 13 -> 17, of which waited for: 8 -> 6; matrix products, arithmetic and copies ran while one was open for 8% -> 7% of each run, Pallas kernels for 37% -> 39%
where the time goes in v2:
time: 90.8 us; the launch traced here: 89.1 us
  Pallas kernels  36.8 us (41%)
  starting transfers between devices  26.9 us (30%)
  waiting for transfers between devices  15.9 us (18%)
  local copies, waits for them, and re-layouts  4.46 us (5%)
  other arithmetic  3.91 us (4%)
  between operations  1.09 us (1%)
    ppermute x16, starting transfers between devices, send(): return lax.ppermute(value, BITS, pairs)  20 us
    pallas_call x2, Pallas kernels, forward(): pl.pallas_call(lambda *refs: forward_kernel(int(bool(rest)), *refs), in_s...  17.5 us
    ppermute x16, waiting for transfers between devices, send(): return lax.ppermute(value, BITS, pairs)  15.9 us
    pallas_call x2, Pallas kernels, grad_half(): pl.pallas_call(lambda *refs: grad_kernel(chunk, *refs), in_specs=[SCALAR,...  14.9 us
    all_to_all x1, starting transfers between devices, local(): lax.all_to_all(mine, BITS, 0, 0, axis_index_groups=quads(), tiled=True)  6.91 us
    unnamed x8, local copies, waits for them, and re-layouts  2.66 us
  transfers between devices with their start and end apart: 17, of which 6 were waited for; matrix products, arithmetic and copies ran while one was open for 7% of the time, Pallas kernels for 39%

profile of v2, /device:TPU:0, one launch (start us, length us, event | category | flops | bytes accessed | tf_op | source)
XLA Modules:
  0.0 89.1 jit_solution(8280928455033904272)
XLA Ops:
  0.7 1.1 %copy-done.1 = bf16[512,512]{1,0:T(8,128)(2,1)S(1)} copy-done((bf16[512,512]{1,0:T(8,128)(2,1)S(1)}, bf16[512,512]{1,0:T(8,128)(2,1)}, u32[]{:S(2)}) %copy-start.1) | copy-done | bytes 524312
  1.9 0.7 copy-done.2
  2.5 0.9 weight.1
  3.4 1.7 %collective-permute-start = (bf16[1,256,512]{2,1,0:T(8,128)(2,1)S(1)}, bf16[1,256,512]{2,1,0:T(8,128)(2,1)S(1)}, u32[]{:S(2)}, u32[]{:S(2)}) collective-permute-start(bf16[1,256,512]{2,1,0:T(8,128)(2,1)S(1)} %weight.1), channel_id=1, source_target_pairs={{0,4},{1,13},{2,6},{3,15},{4,0},{5,9},{6,2},{7,11},{8,12},{9,5},{1... | collective-permute-start | bytes 786440 | tf_op jit(solution)/shard_map/weight_y_near/ppermute | solution.py:52
  5.2 0.7 convert_element_type.63
  5.9 1.0 %multiply_sine_fusion = (f32[64,1024]{1,0:T(8,128)S(1)}, f32[64,1024]{1,0:T(8,128)S(1)}) fusion(f32[1024]{0:T(1024)S(1)} %convert_element_type.63, f32[64]{0:T(128)S(1)} %multiply_power_fusion), kind=kLoop, calls=%fused_computation.23 | loop fusion | flops 65536 | bytes 528640 | tf_op jit(solution)/shard_map/sin | solution.py:273
  6.9 0.9 back.1.refs_1_
  7.8 7.5 %grad.2 = (f32[2,2,2,2,2,64,512]{6,5,4,3,2,1,0:T(8,128)S(1)}, bf16[2,2,2,2,2,64,512]{6,5,4,3,2,1,0:T(8,128)(2,1)S(1)}) custom-call(s32[5]{0:T(128)S(1)} %stack.23.refs_0_.at, bf16[1024,512]{1,0:T(8,128)(2,1)S(1)} %back.1.refs_1_, bf16[1024,8192]{1,0:T(8,128)(2,1)} %refs_1_.3), custom_call_target="tpu_custom_call" | custom-call | flops 42949672960 | bytes 8388608 | tf_op jit(solution)/shard_map/grad/pallas_call | solution.py:135
  15.3 2.0 %collective-permute-start.3 = (bf16[2,256,512]{2,1,0:T(8,128)(2,1)S(1)}, bf16[2,256,512]{2,1,0:T(8,128)(2,1)S(1)}, u32[]{:S(2)}, u32[]{:S(2)}) collective-permute-start(bf16[2,256,512]{2,1,0:T(8,128)(2,1)S(1)} %pad_maximum_fusion), channel_id=1, source_target_pairs={{0,64},{1,67},{2,66},{3,65},{4,68},{5,71},{6,70},{7,69},{8,72},{9,... | collective-permute-start | bytes 1572872 | tf_op jit(solution)/shard_map/weight_z_near/ppermute | solution.py:52
  17.3 2.2 %collective-permute-start.2 = (bf16[2,256,512]{2,1,0:T(8,128)(2,1)S(1)}, bf16[2,256,512]{2,1,0:T(8,128)(2,1)S(1)}, u32[]{:S(2)}, u32[]{:S(2)}) collective-permute-start(bf16[2,256,512]{2,1,0:T(8,128)(2,1)S(1)} %pad_maximum_fusion), channel_id=1, source_target_pairs={{0,12},{1,5},{2,14},{3,7},{4,8},{5,1},{6,10},{7,3},{8,4},{9,13},{1... | collective-permute-start | bytes 1572872 | tf_op jit(solution)/shard_map/weight_y_back/ppermute | solution.py:52
  19.7 0.7 collective-permute-start.1
  20.4 7.5 %grad.3 = (f32[2,2,2,2,2,64,512]{6,5,4,3,2,1,0:T(8,128)S(1)}, bf16[2,2,2,2,2,64,512]{6,5,4,3,2,1,0:T(8,128)(2,1)S(1)}) custom-call(s32[5]{0:T(128)S(1)} %stack.23.refs_0_.at, bf16[1024,512]{1,0:T(8,128)(2,1)S(1)} %back.1.refs_1_, bf16[1024,8192]{1,0:T(8,128)(2,1)} %refs_1_.3), custom_call_target="tpu_custom_call" | custom-call | flops 42949672960 | bytes 8388608 | tf_op jit(solution)/shard_map/grad/pallas_call | solution.py:135
  29.0 1.6 %collective-permute-start.5 = (bf16[2,2,2,2,64,512]{5,4,3,1,0,2:T(8,128)(2,1)S(1)}, bf16[2,2,2,2,64,512]{5,4,3,1,0,2:T(8,128)(2,1)S(1)}, u32[]{:S(2)}, u32[]{:S(2)}) collective-permute-start(bf16[2,2,2,2,64,512]{5,4,3,1,0,2:T(8,128)(2,1)S(1)} %fusion.6), channel_id=1, source_target_pairs={{0,16},{1,49},{2,18},{3,51},{4,20},{5,53},{6,22},{7,55},{8,24},{9,... | collective-permute-start | bytes 3145736 | tf_op jit(solution)/shard_map/far_x/ppermute | solution.py:52
  30.6 2.0 %collective-permute-done.6 = bf16[2,2,2,2,2,64,512]{6,5,4,2,0,1,3:T(8,128)(2,1)S(1)} collective-permute-done((bf16[2,2,2,2,2,64,512]{6,5,4,2,0,1,3:T(8,128)(2,1)S(1)}, bf16[2,2,2,2,2,64,512]{6,5,4,2,0,1,3:T(8,128)(2,1)S(1)}, u32[]{:S(2)}, u32[]{:S(2)}) %collective-permute-start.6) | collective-permute-done | bytes 2097184 | tf_op jit(solution)/shard_map/near_core/ppermute | solution.py:52
  32.9 1.8 %collective-permute-start.7 = (bf16[2,2,2,2,64,512]{5,4,3,2,0,1:T(8,128)(2,1)S(1)}, bf16[2,2,2,2,64,512]{5,4,3,2,0,1:T(8,128)(2,1)S(1)}, u32[]{:S(2)}, u32[]{:S(2)}) collective-permute-start(bf16[2,2,2,2,64,512]{5,4,3,2,0,1:T(8,128)(2,1)S(1)} %fusion.7), channel_id=1, source_target_pairs={{0,4},{1,13},{2,6},{3,15},{4,0},{5,9},{6,2},{7,11},{8,12},{9,5},{1... | collective-permute-start | bytes 3145736 | tf_op jit(solution)/shard_map/near_y/ppermute | solution.py:52
  34.7 0.8 constant_dynamic-update-slice_fusion.3
  35.6 0.8 constant_dynamic-update-slice_fusion.2.refs_2_
  36.4 2.6 %collective-permute-start.13 = (bf16[4,256,512]{2,1,0:T(8,128)(2,1)}, bf16[4,256,512]{2,1,0:T(8,128)(2,1)}, u32[]{:S(2)}, u32[]{:S(2)}) collective-permute-start(bf16[4,256,512]{2,1,0:T(8,128)(2,1)} %constant_dynamic-update-slice_fusion.2.refs_2_), channel_id=1, source_target_pairs={{0,66},{1,65},{2,64},{3,67},{4,70},{5,69},{6,68},{7,71},{8,74},{9,... | collective-permute-start | bytes 3145736 | tf_op jit(solution)/shard_map/weight_z_back/ppermute | solution.py:52
  39.0 4.9 %collective-permute-done.5 = bf16[2,2,2,2,64,512]{5,4,3,1,0,2:T(8,128)(2,1)S(1)} collective-permute-done((bf16[2,2,2,2,64,512]{5,4,3,1,0,2:T(8,128)(2,1)S(1)}, bf16[2,2,2,2,64,512]{5,4,3,1,0,2:T(8,128)(2,1)S(1)}, u32[]{:S(2)}, u32[]{:S(2)}) %collective-permute-start.5) | collective-permute-done | bytes 1048608 | tf_op jit(solution)/shard_map/far_x/ppermute | solution.py:52
  44.1 3.7 %collective-permute-done.7 = bf16[2,2,2,2,64,512]{5,4,3,2,0,1:T(8,128)(2,1)S(1)} collective-permute-done((bf16[2,2,2,2,64,512]{5,4,3,2,0,1:T(8,128)(2,1)S(1)}, bf16[2,2,2,2,64,512]{5,4,3,2,0,1:T(8,128)(2,1)S(1)}, u32[]{:S(2)}, u32[]{:S(2)}) %collective-permute-start.7) | collective-permute-done | bytes 1048608 | tf_op jit(solution)/shard_map/near_y/ppermute | solution.py:52
  48.1 2.4 %collective-permute-start.8 = (bf16[4,256,512]{2,1,0:T(8,128)(2,1)S(1)}, bf16[4,256,512]{2,1,0:T(8,128)(2,1)}, u32[]{:S(2)}, u32[]{:S(2)}) collective-permute-start(bf16[4,256,512]{2,1,0:T(8,128)(2,1)S(1)} %constant_dynamic-update-slice_fusion.refs_3_), channel_id=1, source_target_pairs={{0,66},{1,65},{2,64},{3,67},{4,70},{5,69},{6,68},{7,71},{8,74},{9,... | collective-permute-start | bytes 3145736 | tf_op jit(solution)/shard_map/weight_z_back_late/ppermute | solution.py:52
  50.5 2.1 %collective-permute-start.10 = (bf16[2,2,2,64,512]{4,3,2,1,0:T(8,128)(2,1)S(1)}, bf16[2,2,2,64,512]{4,3,2,1,0:T(8,128)(2,1)S(1)}, u32[]{:S(2)}, u32[]{:S(2)}) collective-permute-start(bf16[2,2,2,64,512]{4,3,2,1,0:T(8,128)(2,1)S(1)} %fusion.13), channel_id=1, source_target_pairs={{0,4},{1,13},{2,6},{3,15},{4,0},{5,9},{6,2},{7,11},{8,12},{9,5},{1... | collective-permute-start | bytes 1572872 | tf_op jit(solution)/shard_map/far_y/ppermute | solution.py:52
  52.6 1.5 %collective-permute-start.9 = (bf16[2,2,2,64,512]{4,3,2,1,0:T(8,128)(2,1)S(1)}, bf16[2,2,2,64,512]{4,3,2,1,0:T(8,128)(2,1)S(1)}, u32[]{:S(2)}, u32[]{:S(2)}) collective-permute-start(bf16[2,2,2,64,512]{4,3,2,1,0:T(8,128)(2,1)S(1)} %fusion.10), channel_id=1, source_target_pairs={{0,16},{1,49},{2,18},{3,51},{4,20},{5,53},{6,22},{7,55},{8,24},{9,... | collective-permute-start | bytes 1572872 | tf_op jit(solution)/shard_map/near_x/ppermute | solution.py:52
  54.7 1.7 %collective-permute-done.13.refs_4_ = bf16[4,256,512]{2,1,0:T(8,128)(2,1)} collective-permute-done((bf16[4,256,512]{2,1,0:T(8,128)(2,1)}, bf16[4,256,512]{2,1,0:T(8,128)(2,1)}, u32[]{:S(2)}, u32[]{:S(2)}) %collective-permute-start.13) | collective-permute-done | bytes 1048608 | tf_op jit(solution)/shard_map/weight_z_back/ppermute | solution.py:52
  57.1 2.6 %collective-permute-done.10.far_in_ref = bf16[2,2,2,64,512]{4,3,2,1,0:T(8,128)(2,1)S(1)} collective-permute-done((bf16[2,2,2,64,512]{4,3,2,1,0:T(8,128)(2,1)S(1)}, bf16[2,2,2,64,512]{4,3,2,1,0:T(8,128)(2,1)S(1)}, u32[]{:S(2)}, u32[]{:S(2)}) %collective-permute-start.10) | collective-permute-done | bytes 524320 | tf_op jit(solution)/shard_map/far_y/ppermute | solution.py:52
  59.7 0.9 %collective-permute-start.12 = (bf16[4,256,512]{2,1,0:T(8,128)(2,1)S(1)}, bf16[4,256,512]{2,1,0:T(8,128)(2,1)}, u32[]{:S(2)}, u32[]{:S(2)}) collective-permute-start(bf16[4,256,512]{2,1,0:T(8,128)(2,1)S(1)} %constant_dynamic-update-slice_fusion.refs_3_), channel_id=1, source_target_pairs={{0,1},{1,0},{2,3},{3,2},{4,5},{5,4},{6,7},{7,6},{8,9},{9,8},{10,11... | collective-permute-start | bytes 3145736 | tf_op jit(solution)/shard_map/weight_core_1/ppermute | solution.py:52
  60.6 1.1 %collective-permute-done.9.near_in_ref = bf16[2,2,2,64,512]{4,3,2,1,0:T(8,128)(2,1)S(1)} collective-permute-done((bf16[2,2,2,64,512]{4,3,2,1,0:T(8,128)(2,1)S(1)}, bf16[2,2,2,64,512]{4,3,2,1,0:T(8,128)(2,1)S(1)}, u32[]{:S(2)}, u32[]{:S(2)}) %collective-permute-start.9) | collective-permute-done | bytes 524320 | tf_op jit(solution)/shard_map/near_x/ppermute | solution.py:52
  61.7 1.7 %sums.1 = bf16[2,2,2,2,64,512]{5,4,3,2,1,0:T(8,128)(2,1)} custom-call(s32[5]{0:T(128)S(1)} %stack.23.refs_0_.at, f32[2,2,2,2,64,512]{5,4,3,2,1,0:T(8,128)S(1)} %copy.15.near_ref, bf16[2,2,2,64,512]{4,3,2,1,0:T(8,128)(2,1)S(1)} %collective-permute-done.9.near_in_ref, f32[2,2,2,2,64,512]{5,4,3,2,1,0:T(8,128)S(1)} %copy.16.far_ref, ...), custom_call_target="tpu_custom_call" | custom-call | tf_op jit(solution)/shard_map/sums/pallas_call | solution.py:253
  63.5 6.9 %all-to-all-start = ((bf16[16,64,512]{2,1,0:T(8,128)(2,1)}), bf16[16,64,512]{2,1,0:T(8,128)(2,1)S(1)}, u32[]{:S(2)}, u32[]{:S(2)}) async-start(bf16[16,64,512]{2,1,0:T(8,128)(2,1)} %bitcast.14), calls=%async_computation | async-start | bytes 2097152 | tf_op jit(solution)/shard_map/all_to_all | solution.py:308
  70.5 7.8 %forward.2.refs_6_ = f32[1024,512]{1,0:T(8,128)S(1)} custom-call(s32[5]{0:T(128)S(1)} %stack.23.refs_0_.at, bf16[1024,8192]{1,0:T(8,128)(2,1)} %refs_1_.3, bf16[4,256,512]{2,1,0:T(8,128)(2,1)} %constant_dynamic-update-slice_fusion.2.refs_2_, bf16[4,256,512]{2,1,0:T(8,128)(2,1)S(1)} %constant_dynamic-update-slice_fusion.refs_3_, ...), custom_call_target="tpu_custom_call" | custom-call | flops 17179869184 | bytes 4194304 | tf_op jit(solution)/shard_map/forward/pallas_call | solution.py:200
  78.3 9.7 %forward.3 = bf16[1024,512]{1,0:T(8,128)(2,1)} custom-call(s32[5]{0:T(128)S(1)} %stack.23.refs_0_.at, bf16[1024,8192]{1,0:T(8,128)(2,1)} %refs_1_.3, bf16[4,256,512]{2,1,0:T(8,128)(2,1)} %collective-permute-done.11.refs_2_, bf16[4,256,512]{2,1,0:T(8,128)(2,1)} %collective-permute-done.12.refs_3_, bf16[4,256,512]{2,1,0:T(8,128)(2,1)} %collective-permute-done.14.refs_4_, ...), custom_call_target="tpu_custom_call" | custom-call | flops 17179869184 | bytes 4194304 | tf_op jit(solution)/shard_map/forward/pallas_call | solution.py:200
  88.1 0.9 %total.1 = f32[64,512]{1,0:T(8,128)} custom-call(bf16[16,64,512]{2,1,0:T(8,128)(2,1)S(1)} %all-to-all-done.got_ref), custom_call_target="tpu_custom_call" | custom-call | tf_op jit(solution)/shard_map/total/pallas_call | solution.py:232
  (35 shorter events, 3.9 us)
Async XLA Ops:
  0.6 6.2 %copy-start = (bf16[1024,512]{1,0:T(8,128)(2,1)S(1)}, bf16[1024,512]{1,0:T(8,128)(2,1)}, u32[]{:S(2)}) copy-start(bf16[1024,512]{1,0:T(8,128)(2,1)} %cotangent_ref.1) | copy-start | bytes 3145732
  0.7 1.1 %copy-start.1 = (bf16[512,512]{1,0:T(8,128)(2,1)S(1)}, bf16[512,512]{1,0:T(8,128)(2,1)}, u32[]{:S(2)}) copy-start(bf16[512,512]{1,0:T(8,128)(2,1)} %codes_ref.1) | copy-start | bytes 1572868
  1.9 0.7 copy-start.2
  3.4 11.8 %collective-permute-start = (bf16[1,256,512]{2,1,0:T(8,128)(2,1)S(1)}, bf16[1,256,512]{2,1,0:T(8,128)(2,1)S(1)}, u32[]{:S(2)}, u32[]{:S(2)}) collective-permute-start(bf16[1,256,512]{2,1,0:T(8,128)(2,1)S(1)} %weight.1), channel_id=1, source_target_pairs={{0,4},{1,13},{2,6},{3,15},{4,0},{5,9},{6,2},{7,11},{8,12},{9,5},{1... | collective-permute-start | bytes 786440 | tf_op jit(solution)/shard_map/weight_y_near/ppermute | solution.py:52
  15.3 12.6 %collective-permute-start.3 = (bf16[2,256,512]{2,1,0:T(8,128)(2,1)S(1)}, bf16[2,256,512]{2,1,0:T(8,128)(2,1)S(1)}, u32[]{:S(2)}, u32[]{:S(2)}) collective-permute-start(bf16[2,256,512]{2,1,0:T(8,128)(2,1)S(1)} %pad_maximum_fusion), channel_id=1, source_target_pairs={{0,64},{1,67},{2,66},{3,65},{4,68},{5,71},{6,70},{7,69},{8,72},{9,... | collective-permute-start | bytes 1572872 | tf_op jit(solution)/shard_map/weight_z_near/ppermute | solution.py:52
  17.3 10.6 %collective-permute-start.2 = (bf16[2,256,512]{2,1,0:T(8,128)(2,1)S(1)}, bf16[2,256,512]{2,1,0:T(8,128)(2,1)S(1)}, u32[]{:S(2)}, u32[]{:S(2)}) collective-permute-start(bf16[2,256,512]{2,1,0:T(8,128)(2,1)S(1)} %pad_maximum_fusion), channel_id=1, source_target_pairs={{0,12},{1,5},{2,14},{3,7},{4,8},{5,1},{6,10},{7,3},{8,4},{9,13},{1... | collective-permute-start | bytes 1572872 | tf_op jit(solution)/shard_map/weight_y_back/ppermute | solution.py:52
  19.7 8.2 %collective-permute-start.1 = (bf16[2,2,2,2,2,64,512]{6,5,4,2,0,3,1:T(8,128)(2,1)S(1)}, bf16[2,2,2,2,2,64,512]{6,5,4,2,0,3,1:T(8,128)(2,1)S(1)}, u32[]{:S(2)}, u32[]{:S(2)}) collective-permute-start(bf16[2,2,2,2,2,64,512]{6,5,4,2,0,3,1:T(8,128)(2,1)S(1)} %copy.7), channel_id=1, source_target_pairs={{0,1},{1,0},{2,3},{3,2},{4,5},{5,4},{6,7},{7,6},{8,9},{9,8},{10,11... | collective-permute-start | bytes 6291464 | tf_op jit(solution)/shard_map/far_core/ppermute | solution.py:52
  28.1 4.4 %collective-permute-start.6 = (bf16[2,2,2,2,2,64,512]{6,5,4,2,0,1,3:T(8,128)(2,1)S(1)}, bf16[2,2,2,2,2,64,512]{6,5,4,2,0,1,3:T(8,128)(2,1)S(1)}, u32[]{:S(2)}, u32[]{:S(2)}) collective-permute-start(bf16[2,2,2,2,2,64,512]{6,5,4,2,0,1,3:T(8,128)(2,1)S(1)} %copy.11), channel_id=1, source_target_pairs={{0,1},{1,0},{2,3},{3,2},{4,5},{5,4},{6,7},{7,6},{8,9},{9,8},{10,11... | collective-permute-start | bytes 6291464 | tf_op jit(solution)/shard_map/near_core/ppermute | solution.py:52
  29.0 14.9 %collective-permute-start.5 = (bf16[2,2,2,2,64,512]{5,4,3,1,0,2:T(8,128)(2,1)S(1)}, bf16[2,2,2,2,64,512]{5,4,3,1,0,2:T(8,128)(2,1)S(1)}, u32[]{:S(2)}, u32[]{:S(2)}) collective-permute-start(bf16[2,2,2,2,64,512]{5,4,3,1,0,2:T(8,128)(2,1)S(1)} %fusion.6), channel_id=1, source_target_pairs={{0,16},{1,49},{2,18},{3,51},{4,20},{5,53},{6,22},{7,55},{8,24},{9,... | collective-permute-start | bytes 3145736 | tf_op jit(solution)/shard_map/far_x/ppermute | solution.py:52
  32.9 14.9 %collective-permute-start.7 = (bf16[2,2,2,2,64,512]{5,4,3,2,0,1:T(8,128)(2,1)S(1)}, bf16[2,2,2,2,64,512]{5,4,3,2,0,1:T(8,128)(2,1)S(1)}, u32[]{:S(2)}, u32[]{:S(2)}) collective-permute-start(bf16[2,2,2,2,64,512]{5,4,3,2,0,1:T(8,128)(2,1)S(1)} %fusion.7), channel_id=1, source_target_pairs={{0,4},{1,13},{2,6},{3,15},{4,0},{5,9},{6,2},{7,11},{8,12},{9,5},{1... | collective-permute-start | bytes 3145736 | tf_op jit(solution)/shard_map/near_y/ppermute | solution.py:52
  35.6 12.5 %collective-permute-start.4 = (bf16[2,256,512]{2,1,0:T(8,128)(2,1)S(1)}, bf16[2,256,512]{2,1,0:T(8,128)(2,1)S(1)}, u32[]{:S(2)}, u32[]{:S(2)}) collective-permute-start(bf16[2,256,512]{2,1,0:T(8,128)(2,1)S(1)} %collective-permute-done.2), channel_id=1, source_target_pairs={{0,64},{1,67},{2,66},{3,65},{4,68},{5,71},{6,70},{7,69},{8,72},{9,... | collective-permute-start | bytes 1572872 | tf_op jit(solution)/shard_map/weight_z_near_late/ppermute | solution.py:52
  36.4 20.0 %collective-permute-start.13 = (bf16[4,256,512]{2,1,0:T(8,128)(2,1)}, bf16[4,256,512]{2,1,0:T(8,128)(2,1)}, u32[]{:S(2)}, u32[]{:S(2)}) collective-permute-start(bf16[4,256,512]{2,1,0:T(8,128)(2,1)} %constant_dynamic-update-slice_fusion.2.refs_2_), channel_id=1, source_target_pairs={{0,66},{1,65},{2,64},{3,67},{4,70},{5,69},{6,68},{7,71},{8,74},{9,... | collective-permute-start | bytes 3145736 | tf_op jit(solution)/shard_map/weight_z_back/ppermute | solution.py:52
  48.1 22.3 %collective-permute-start.8 = (bf16[4,256,512]{2,1,0:T(8,128)(2,1)S(1)}, bf16[4,256,512]{2,1,0:T(8,128)(2,1)}, u32[]{:S(2)}, u32[]{:S(2)}) collective-permute-start(bf16[4,256,512]{2,1,0:T(8,128)(2,1)S(1)} %constant_dynamic-update-slice_fusion.refs_3_), channel_id=1, source_target_pairs={{0,66},{1,65},{2,64},{3,67},{4,70},{5,69},{6,68},{7,71},{8,74},{9,... | collective-permute-start | bytes 3145736 | tf_op jit(solution)/shard_map/weight_z_back_late/ppermute | solution.py:52
  50.5 27.8 %collective-permute-start.11 = (bf16[4,256,512]{2,1,0:T(8,128)(2,1)}, bf16[4,256,512]{2,1,0:T(8,128)(2,1)}, u32[]{:S(2)}, u32[]{:S(2)}) collective-permute-start(bf16[4,256,512]{2,1,0:T(8,128)(2,1)} %constant_dynamic-update-slice_fusion.2.refs_2_), channel_id=1, source_target_pairs={{0,1},{1,0},{2,3},{3,2},{4,5},{5,4},{6,7},{7,6},{8,9},{9,8},{10,11... | collective-permute-start | bytes 3145736 | tf_op jit(solution)/shard_map/weight_core_0/ppermute | solution.py:52
  50.5 9.2 %collective-permute-start.10 = (bf16[2,2,2,64,512]{4,3,2,1,0:T(8,128)(2,1)S(1)}, bf16[2,2,2,64,512]{4,3,2,1,0:T(8,128)(2,1)S(1)}, u32[]{:S(2)}, u32[]{:S(2)}) collective-permute-start(bf16[2,2,2,64,512]{4,3,2,1,0:T(8,128)(2,1)S(1)} %fusion.13), channel_id=1, source_target_pairs={{0,4},{1,13},{2,6},{3,15},{4,0},{5,9},{6,2},{7,11},{8,12},{9,5},{1... | collective-permute-start | bytes 1572872 | tf_op jit(solution)/shard_map/far_y/ppermute | solution.py:52
  52.6 9.2 %collective-permute-start.9 = (bf16[2,2,2,64,512]{4,3,2,1,0:T(8,128)(2,1)S(1)}, bf16[2,2,2,64,512]{4,3,2,1,0:T(8,128)(2,1)S(1)}, u32[]{:S(2)}, u32[]{:S(2)}) collective-permute-start(bf16[2,2,2,64,512]{4,3,2,1,0:T(8,128)(2,1)S(1)} %fusion.10), channel_id=1, source_target_pairs={{0,16},{1,49},{2,18},{3,51},{4,20},{5,53},{6,22},{7,55},{8,24},{9,... | collective-permute-start | bytes 1572872 | tf_op jit(solution)/shard_map/near_x/ppermute | solution.py:52
  56.4 21.9 %collective-permute-start.14 = (bf16[4,256,512]{2,1,0:T(8,128)(2,1)}, bf16[4,256,512]{2,1,0:T(8,128)(2,1)}, u32[]{:S(2)}, u32[]{:S(2)}) collective-permute-start(bf16[4,256,512]{2,1,0:T(8,128)(2,1)} %collective-permute-done.13.refs_4_), channel_id=1, source_target_pairs={{0,1},{1,0},{2,3},{3,2},{4,5},{5,4},{6,7},{7,6},{8,9},{9,8},{10,11... | collective-permute-start | bytes 3145736 | tf_op jit(solution)/shard_map/weight_core_2/ppermute | solution.py:52
  59.7 18.6 %collective-permute-start.12 = (bf16[4,256,512]{2,1,0:T(8,128)(2,1)S(1)}, bf16[4,256,512]{2,1,0:T(8,128)(2,1)}, u32[]{:S(2)}, u32[]{:S(2)}) collective-permute-start(bf16[4,256,512]{2,1,0:T(8,128)(2,1)S(1)} %constant_dynamic-update-slice_fusion.refs_3_), channel_id=1, source_target_pairs={{0,1},{1,0},{2,3},{3,2},{4,5},{5,4},{6,7},{7,6},{8,9},{9,8},{10,11... | collective-permute-start | bytes 3145736 | tf_op jit(solution)/shard_map/weight_core_1/ppermute | solution.py:52
  63.5 24.6 %all-to-all-start = ((bf16[16,64,512]{2,1,0:T(8,128)(2,1)}), bf16[16,64,512]{2,1,0:T(8,128)(2,1)S(1)}, u32[]{:S(2)}, u32[]{:S(2)}) async-start(bf16[16,64,512]{2,1,0:T(8,128)(2,1)} %bitcast.14), calls=%async_computation | async-start | bytes 2097152 | tf_op jit(solution)/shard_map/all_to_all | solution.py:308
  70.4 7.9 %collective-permute-start.15 = (bf16[4,256,512]{2,1,0:T(8,128)(2,1)}, bf16[4,256,512]{2,1,0:T(8,128)(2,1)S(1)}, u32[]{:S(2)}, u32[]{:S(2)}) collective-permute-start(bf16[4,256,512]{2,1,0:T(8,128)(2,1)} %collective-permute-done.8.refs_5_), channel_id=1, source_target_pairs={{0,1},{1,0},{2,3},{3,2},{4,5},{5,4},{6,7},{7,6},{8,9},{9,8},{10,11... | collective-permute-start | bytes 3145736 | tf_op jit(solution)/shard_map/weight_core_3/ppermute | solution.py:52

commit v3 on v2

--- a/solution.py
+++ b/solution.py
@@ -14,7 +14,6 @@
 BITS = ("zlo", "xhi", "xlo", "yhi", "ylo", "zhi", "core")
 LIMIT = 8 * MIB
 LARGE = 36 * MIB
-COVER = 4
 VMEM = pl.BlockSpec(memory_space=pltpu.VMEM)
 SCALAR = pl.BlockSpec(memory_space=pltpu.SMEM)
 NEAR, BACK = (1, 3), (3, 1)
@@ -52,9 +51,8 @@
         return lax.ppermute(value, BITS, pairs)
 
 
-def held_at(distance, core):
-    near = jnp.where(core == 0, 1, 3)
-    return jnp.where(distance == 0, 0, jnp.where(distance == 2, 3, jnp.where(distance == near, 1, 2)))
+def held_from(place, core):
+    return jnp.where(core == 0, *(((0, 0), (1, 3), (3, 1), (2, 2))[place]))
 
 
 def weight_kernel(at, codes_ref, scales_ref, piece_ref, scaled):
@@ -147,72 +145,60 @@
     )(at, back, tokens)
 
 
-def forward_kernel(other, at, tokens_ref, *rest):
+def forward_kernel(parts, count, at, tokens_ref, *rest):
     y, zlo, zhi, core = at[1], at[2], at[3], at[4]
-    parts, rest = rest[:4], rest[4:]
-    acc, weight, block, arrived, filled = rest[-5:]
-    holder = core ^ other
-
-    def fetch(i):
-        column = pl.multiple_of((2 * i + holder) * 512, 512)
-        return pltpu.make_async_copy(tokens_ref.at[:, pl.ds(column, 512)], block.at[i], arrived.at[i])
-
-    def fill(i, to_zlo, ref, place):
-        rows = pl.ds(to_zlo * 256, 256)
-        return pltpu.make_async_copy(ref.at[place], weight.at[i, rows], filled.at[2 * i + to_zlo])
-
-    def start_fill(i, to_zlo):
-        from_y = held_at(y ^ (i // 2), holder)
-        from_z = held_at((2 * zhi + zlo) ^ (2 * (i % 2) + to_zlo), holder)
-        for n, ref in enumerate(parts):
-
-            @pl.when((from_z // 2) * 2 + from_y // 2 == n)
-            def _():
-                fill(i, to_zlo, ref, (from_z % 2) * 2 + from_y % 2).start()
-
-    for i in range(8):
-        fetch(i).start()
-        start_fill(i, 0)
-        start_fill(i, 1)
-    acc[...] = rest[0][...] if other else jnp.zeros_like(acc)
-
-    @pl.loop(0, 8)
-    def _(i):
-        fetch(i).wait()
-        fill(i, 0, parts[0], 0).wait()
-        fill(i, 1, parts[0], 0).wait()
-        acc[...] += jnp.dot(block[i], weight[i], preferred_element_type=F32)
-
-    if other:
+    weights, rest = rest[:count], rest[count:]
+    block, arrived = rest[-2:]
+
+    def fetch(n, quarter):
+        z_half, y_half, other, _, _ = parts[n]
+        holder = core ^ other
+        to_y = y ^ held_from(2 * y_half + quarter % 2, holder)
+        to_z = (2 * zhi + zlo) ^ held_from(2 * z_half + quarter // 2, holder)
+        column = ((to_y * 2 + to_z // 2) * 2 + holder) * 512 + (to_z % 2) * 256
+        return pltpu.make_async_copy(
+            tokens_ref.at[:, pl.ds(pl.multiple_of(column, 256), 256)],
+            block.at[n, :, quarter * 256 : (quarter + 1) * 256],
+            arrived.at[n, quarter],
+        )
+
+    for n in range(len(parts)):
+        for quarter in range(4):
+            fetch(n, quarter).start()
+    total = rest[0] if len(rest) > 3 else None
+    out = rest[-3]
+    for n, (_, _, _, place, start) in enumerate(parts):
+        for quarter in range(4):
+            fetch(n, quarter).wait()
+        weight = weights[place][start : start + 4].reshape(1024, 512)
+        product = jnp.dot(block[n], weight, preferred_element_type=F32)
+        out[...] = product if total is None else total[...] + product
+        total = out
+    if len(rest) > 4:
         cos, sin = head_turn(*rest[1:3])
         keys_ref = rest[3]
         for head in range(4):
-            raw = acc[:, head * HD : (head + 1) * HD]
+            raw = out[:, head * HD : (head + 1) * HD]
             turned = pltpu.roll(raw, HALF, 1)
             keys_ref[:, head * HD : (head + 1) * HD] = (raw * cos + turned * sin).astype(BF16)
 
 
-def forward(at, tokens, parts, *rest):
-    rows, depth = tokens.shape
-    width = parts[0].shape[-1]
-    hbm = pl.BlockSpec(memory_space=pltpu.HBM)
+def forward(at, tokens, parts, weights, *rest, cover=1):
+    rows, _ = tokens.shape
+    width = weights[0].shape[-1]
+    last = len(rest) == 3
     total = pltpu.VMEM((rows, width), F32)
     return pl.pallas_call(
-        lambda *refs: forward_kernel(int(bool(rest)), *refs),
-        in_specs=[SCALAR] + [hbm] * 5 + [VMEM] * len(rest),
-        out_specs=VMEM,
-        scratch_shapes=[total] * bool(rest)
-        + [
-            pltpu.VMEM((8, 512, width), BF16),
-            pltpu.VMEM((8, rows, 512), BF16),
-            pltpu.SemaphoreType.DMA((8,)),
-            pltpu.SemaphoreType.DMA((16,)),
-        ],
-        out_shape=jax.ShapeDtypeStruct((rows, width), BF16 if rest else F32),
+        lambda *refs: forward_kernel(parts, len(weights), *refs),
+        in_specs=[SCALAR, pl.BlockSpec(memory_space=pltpu.HBM)] + [VMEM] * (len(weights) + len(rest)),
+        out_specs=VMEM,
+        scratch_shapes=[total] * last
+        + [pltpu.VMEM((len(parts), rows, 1024), BF16), pltpu.SemaphoreType.DMA((len(parts), 4))],
+        out_shape=jax.ShapeDtypeStruct((rows, width), BF16 if last else F32),
         compiler_params=pltpu.CompilerParams(vmem_limit_bytes=LARGE),
-        cost_estimate=pl.CostEstimate(flops=COVER * rows * depth * width, bytes_accessed=4 * MIB, transcendentals=0),
+        cost_estimate=pl.CostEstimate(flops=cover * rows * 1024 * width, bytes_accessed=MIB, transcendentals=0),
         name="forward",
-    )(at, tokens, *parts, *rest)
+    )(at, tokens, *weights, *rest)
 
 
 def total_kernel(got_ref, out_ref, block, arrived):
@@ -303,13 +289,25 @@
     part_got, _, _ = tie((part_got, far_sent, near_sent))
     parts.append(jnp.concatenate([weight_got, part_got]))
     late.append(send("weight_z_back_late", parts[1], z=BACK))
-    sib += [send("weight_core_1", parts[1], core=(1, 1)), send("weight_core_2", late[0], core=(1, 1))]
+    sib += [send("weight_core_1", parts[1], core=(1, 1))]
+    at, _, _ = tie((at, far_sent, near_sent))
+    half = forward(
+        at, tokens, [(0, 0, 0, 0, 0), (0, 0, 1, 1, 0)], [parts[0], sib[0]], cover=24
+    )
+    half, far_in, near_in = tie((half, far_in, near_in))
     mine = sums(at, near, near_in, far, far_in).reshape(16, 64, 512)
     got = lax.all_to_all(mine, BITS, 0, 0, axis_index_groups=quads(), tiled=True)
-    at, late[1], _ = tie((at, late[1], mine))
-    sib.append(send("weight_core_3", late[1], core=(1, 1)))
-    half = forward(at, tokens, parts + late)
-    keys = forward(at, tokens, sib, half, cos, sin)
+    at, late[0], late[1], _ = tie((at, late[0], late[1], mine))
+    sib += [send("weight_core_2", late[0], core=(1, 1)), send("weight_core_3", late[1], core=(1, 1))]
+    half = forward(
+        at,
+        tokens,
+        [(0, 1, 0, 0, 0), (1, 0, 0, 1, 0), (1, 1, 0, 2, 0), (0, 1, 1, 3, 0)],
+        [parts[1], late[0], late[1], sib[1]],
+        half,
+        cover=32,
+    )
+    keys = forward(at, tokens, [(1, 0, 1, 0, 0), (1, 1, 1, 1, 0)], [sib[2], sib[3]], half, cos, sin, cover=16)
     keys, got = tie((keys, got))
     return keys, total_of(got)
 

time: 90.8 us -> 89.1 us (0.981)
  waiting for transfers between devices: 15.9 us -> 11.7 us
  local copies, waits for them, and re-layouts: 4.46 us -> 6.86 us
  Pallas kernels: 36.8 us -> 38.9 us
  starting transfers between devices: 26.9 us -> 25.3 us
    ppermute x16, waiting for transfers between devices: 15.9 us -> 11.7 us  [send(): return lax.ppermute(value, BITS, pairs)]
    unnamed x8 -> x12, local copies, waits for them, and re-layouts: 2.66 us -> 5.1 us
    pallas_call x2 -> x3, Pallas kernels: 17.5 us -> 19.6 us  [forward(): pl.pallas_call(lambda *refs: forward_kernel(parts, len(weights), *refs),...]
    all_to_all x1, starting transfers between devices: 6.91 us -> 5.68 us  [local(): lax.all_to_all(mine, BITS, 0, 0, axis_index_groups=quads(), tiled=True)]
  transfers between devices with their start and end apart: 17 -> 17, of which waited for: 6 -> 5; matrix products, arithmetic and copies ran while one was open for 7% -> 7% of each run, Pallas kernels for 39% -> 42%
where the time goes in v3:
time: 89.1 us; the launch traced here: 87.8 us
  Pallas kernels  38.9 us (44%)
  starting transfers between devices  25.3 us (28%)
  waiting for transfers between devices  11.7 us (13%)
  local copies, waits for them, and re-layouts  6.86 us (8%)
  other arithmetic  3.9 us (4%)
  between operations  1.1 us (1%)
    ppermute x16, starting transfers between devices, send(): return lax.ppermute(value, BITS, pairs)  19.6 us
    pallas_call x3, Pallas kernels, forward(): pl.pallas_call(lambda *refs: forward_kernel(parts, len(weights), *refs),...  19.6 us
    pallas_call x2, Pallas kernels, grad_half(): pl.pallas_call(lambda *refs: grad_kernel(chunk, *refs), in_specs=[SCALAR,...  14.9 us
    ppermute x16, waiting for transfers between devices, send(): return lax.ppermute(value, BITS, pairs)  11.7 us
    all_to_all x1, starting transfers between devices, local(): lax.all_to_all(mine, BITS, 0, 0, axis_index_groups=quads(), tiled=True)  5.68 us
    unnamed x12, local copies, waits for them, and re-layouts  5.1 us
  transfers between devices with their start and end apart: 17, of which 5 were waited for; matrix products, arithmetic and copies ran while one was open for 7% of the time, Pallas kernels for 42%

profile of v3, /device:TPU:0, one launch (start us, length us, event | category | flops | bytes accessed | tf_op | source)
XLA Modules:
  0.0 87.8 jit_solution(7836782866753285598)
XLA Ops:
  0.7 1.1 %copy-done.1 = bf16[512,512]{1,0:T(8,128)(2,1)S(1)} copy-done((bf16[512,512]{1,0:T(8,128)(2,1)S(1)}, bf16[512,512]{1,0:T(8,128)(2,1)}, u32[]{:S(2)}) %copy-start.1) | copy-done | bytes 524312
  2.5 0.9 %weight.1 = bf16[1,256,512]{2,1,0:T(8,128)(2,1)S(1)} custom-call(s32[5]{0:T(128)S(1)} %stack.23.refs_0_.at, bf16[512,512]{1,0:T(8,128)(2,1)S(1)} %copy-done.1, f32[2,512]{1,0:T(2,128)S(1)} %bitcast.41), custom_call_target="tpu_custom_call" | custom-call | tf_op jit(solution)/shard_map/weight/pallas_call | solution.py:68
  3.4 1.7 %collective-permute-start = (bf16[1,256,512]{2,1,0:T(8,128)(2,1)S(1)}, bf16[1,256,512]{2,1,0:T(8,128)(2,1)S(1)}, u32[]{:S(2)}, u32[]{:S(2)}) collective-permute-start(bf16[1,256,512]{2,1,0:T(8,128)(2,1)S(1)} %weight.1), channel_id=1, source_target_pairs={{0,4},{1,13},{2,6},{3,15},{4,0},{5,9},{6,2},{7,11},{8,12},{9,5},{1... | collective-permute-start | bytes 786440 | tf_op jit(solution)/shard_map/weight_y_near/ppermute | solution.py:51
  5.2 0.7 convert_element_type.63
  5.9 1.0 %multiply_sine_fusion = (f32[64,1024]{1,0:T(8,128)S(1)}, f32[64,1024]{1,0:T(8,128)S(1)}) fusion(f32[1024]{0:T(1024)S(1)} %convert_element_type.63, f32[64]{0:T(128)S(1)} %multiply_power_fusion), kind=kLoop, calls=%fused_computation.23 | loop fusion | flops 65536 | bytes 528640 | tf_op jit(solution)/shard_map/sin | solution.py:259
  6.9 0.9 back.1.refs_1_
  7.8 7.5 %grad.2 = (f32[2,2,2,2,2,64,512]{6,5,4,3,2,1,0:T(8,128)S(1)}, bf16[2,2,2,2,2,64,512]{6,5,4,3,2,1,0:T(8,128)(2,1)S(1)}) custom-call(s32[5]{0:T(128)S(1)} %stack.23.refs_0_.at, bf16[1024,512]{1,0:T(8,128)(2,1)S(1)} %back.1.refs_1_, bf16[1024,8192]{1,0:T(8,128)(2,1)} %refs_1_.5), custom_call_target="tpu_custom_call" | custom-call | flops 42949672960 | bytes 8388608 | tf_op jit(solution)/shard_map/grad/pallas_call | solution.py:133
  15.3 2.0 %collective-permute-start.3 = (bf16[2,256,512]{2,1,0:T(8,128)(2,1)S(1)}, bf16[2,256,512]{2,1,0:T(8,128)(2,1)S(1)}, u32[]{:S(2)}, u32[]{:S(2)}) collective-permute-start(bf16[2,256,512]{2,1,0:T(8,128)(2,1)S(1)} %pad_maximum_fusion), channel_id=1, source_target_pairs={{0,64},{1,67},{2,66},{3,65},{4,68},{5,71},{6,70},{7,69},{8,72},{9,... | collective-permute-start | bytes 1572872 | tf_op jit(solution)/shard_map/weight_z_near/ppermute | solution.py:51
  17.3 2.2 %collective-permute-start.2 = (bf16[2,256,512]{2,1,0:T(8,128)(2,1)S(1)}, bf16[2,256,512]{2,1,0:T(8,128)(2,1)S(1)}, u32[]{:S(2)}, u32[]{:S(2)}) collective-permute-start(bf16[2,256,512]{2,1,0:T(8,128)(2,1)S(1)} %pad_maximum_fusion), channel_id=1, source_target_pairs={{0,12},{1,5},{2,14},{3,7},{4,8},{5,1},{6,10},{7,3},{8,4},{9,13},{1... | collective-permute-start | bytes 1572872 | tf_op jit(solution)/shard_map/weight_y_back/ppermute | solution.py:51
  19.7 0.7 collective-permute-start.1
  20.4 7.5 %grad.3 = (f32[2,2,2,2,2,64,512]{6,5,4,3,2,1,0:T(8,128)S(1)}, bf16[2,2,2,2,2,64,512]{6,5,4,3,2,1,0:T(8,128)(2,1)S(1)}) custom-call(s32[5]{0:T(128)S(1)} %stack.23.refs_0_.at, bf16[1024,512]{1,0:T(8,128)(2,1)S(1)} %back.1.refs_1_, bf16[1024,8192]{1,0:T(8,128)(2,1)} %refs_1_.5), custom_call_target="tpu_custom_call" | custom-call | flops 42949672960 | bytes 8388608 | tf_op jit(solution)/shard_map/grad/pallas_call | solution.py:133
  29.0 1.6 %collective-permute-start.4 = (bf16[2,2,2,2,64,512]{5,4,3,1,0,2:T(8,128)(2,1)S(1)}, bf16[2,2,2,2,64,512]{5,4,3,1,0,2:T(8,128)(2,1)S(1)}, u32[]{:S(2)}, u32[]{:S(2)}) collective-permute-start(bf16[2,2,2,2,64,512]{5,4,3,1,0,2:T(8,128)(2,1)S(1)} %fusion.6), channel_id=1, source_target_pairs={{0,16},{1,49},{2,18},{3,51},{4,20},{5,53},{6,22},{7,55},{8,24},{9,... | collective-permute-start | bytes 3145736 | tf_op jit(solution)/shard_map/far_x/ppermute | solution.py:51
  30.6 2.0 %collective-permute-done.5 = bf16[2,2,2,2,2,64,512]{6,5,4,2,0,1,3:T(8,128)(2,1)S(1)} collective-permute-done((bf16[2,2,2,2,2,64,512]{6,5,4,2,0,1,3:T(8,128)(2,1)S(1)}, bf16[2,2,2,2,2,64,512]{6,5,4,2,0,1,3:T(8,128)(2,1)S(1)}, u32[]{:S(2)}, u32[]{:S(2)}) %collective-permute-start.5) | collective-permute-done | bytes 2097184 | tf_op jit(solution)/shard_map/near_core/ppermute | solution.py:51
  32.9 1.8 %collective-permute-start.6 = (bf16[2,2,2,2,64,512]{5,4,3,2,0,1:T(8,128)(2,1)S(1)}, bf16[2,2,2,2,64,512]{5,4,3,2,0,1:T(8,128)(2,1)S(1)}, u32[]{:S(2)}, u32[]{:S(2)}) collective-permute-start(bf16[2,2,2,2,64,512]{5,4,3,2,0,1:T(8,128)(2,1)S(1)} %fusion.7), channel_id=1, source_target_pairs={{0,4},{1,13},{2,6},{3,15},{4,0},{5,9},{6,2},{7,11},{8,12},{9,5},{1... | collective-permute-start | bytes 3145736 | tf_op jit(solution)/shard_map/near_y/ppermute | solution.py:51
  34.7 0.8 constant_dynamic-update-slice_fusion.1
  35.6 0.8 constant_dynamic-update-slice_fusion.refs_2_
  36.5 2.5 %collective-permute-start.7 = (bf16[4,256,512]{2,1,0:T(8,128)(2,1)}, bf16[4,256,512]{2,1,0:T(8,128)(2,1)}, u32[]{:S(2)}, u32[]{:S(2)}) collective-permute-start(bf16[4,256,512]{2,1,0:T(8,128)(2,1)} %constant_dynamic-update-slice_fusion.refs_2_), channel_id=1, source_target_pairs={{0,66},{1,65},{2,64},{3,67},{4,70},{5,69},{6,68},{7,71},{8,74},{9,... | collective-permute-start | bytes 3145736 | tf_op jit(solution)/shard_map/weight_z_back/ppermute | solution.py:51
  39.0 1.0 %collective-permute-start.8 = (bf16[2,256,512]{2,1,0:T(8,128)(2,1)S(1)}, bf16[2,256,512]{2,1,0:T(8,128)(2,1)S(1)}, u32[]{:S(2)}, u32[]{:S(2)}) collective-permute-start(bf16[2,256,512]{2,1,0:T(8,128)(2,1)S(1)} %collective-permute-done.2), channel_id=1, source_target_pairs={{0,64},{1,67},{2,66},{3,65},{4,68},{5,71},{6,70},{7,69},{8,72},{9,... | collective-permute-start | bytes 1572872 | tf_op jit(solution)/shard_map/weight_z_near_late/ppermute | solution.py:51
  40.1 3.8 %collective-permute-done.4 = bf16[2,2,2,2,64,512]{5,4,3,1,0,2:T(8,128)(2,1)S(1)} collective-permute-done((bf16[2,2,2,2,64,512]{5,4,3,1,0,2:T(8,128)(2,1)S(1)}, bf16[2,2,2,2,64,512]{5,4,3,1,0,2:T(8,128)(2,1)S(1)}, u32[]{:S(2)}, u32[]{:S(2)}) %collective-permute-start.4) | collective-permute-done | bytes 1048608 | tf_op jit(solution)/shard_map/far_x/ppermute | solution.py:51
  44.8 1.6 %collective-permute-start.11 = (bf16[2,2,2,64,512]{4,3,2,1,0:T(8,128)(2,1)S(1)}, bf16[2,2,2,64,512]{4,3,2,1,0:T(8,128)(2,1)S(1)}, u32[]{:S(2)}, u32[]{:S(2)}) collective-permute-start(bf16[2,2,2,64,512]{4,3,2,1,0:T(8,128)(2,1)S(1)} %fusion.13), channel_id=1, source_target_pairs={{0,4},{1,13},{2,6},{3,15},{4,0},{5,9},{6,2},{7,11},{8,12},{9,5},{1... | collective-permute-start | bytes 1572872 | tf_op jit(solution)/shard_map/far_y/ppermute | solution.py:51
  46.4 1.4 %collective-permute-done.6 = bf16[2,2,2,2,64,512]{5,4,3,2,0,1:T(8,128)(2,1)S(1)} collective-permute-done((bf16[2,2,2,2,64,512]{5,4,3,2,0,1:T(8,128)(2,1)S(1)}, bf16[2,2,2,2,64,512]{5,4,3,2,0,1:T(8,128)(2,1)S(1)}, u32[]{:S(2)}, u32[]{:S(2)}) %collective-permute-start.6) | collective-permute-done | bytes 1048608 | tf_op jit(solution)/shard_map/near_y/ppermute | solution.py:51
  48.0 1.6 %collective-permute-start.12 = (bf16[2,2,2,64,512]{4,3,2,1,0:T(8,128)(2,1)S(1)}, bf16[2,2,2,64,512]{4,3,2,1,0:T(8,128)(2,1)S(1)}, u32[]{:S(2)}, u32[]{:S(2)}) collective-permute-start(bf16[2,2,2,64,512]{4,3,2,1,0:T(8,128)(2,1)S(1)} %fusion.10), channel_id=1, source_target_pairs={{0,16},{1,49},{2,18},{3,51},{4,20},{5,53},{6,22},{7,55},{8,24},{9,... | collective-permute-start | bytes 1572872 | tf_op jit(solution)/shard_map/near_x/ppermute | solution.py:51
  49.6 4.2 %collective-permute-done.8 = bf16[2,256,512]{2,1,0:T(8,128)(2,1)S(1)} collective-permute-done((bf16[2,256,512]{2,1,0:T(8,128)(2,1)S(1)}, bf16[2,256,512]{2,1,0:T(8,128)(2,1)S(1)}, u32[]{:S(2)}, u32[]{:S(2)}) %collective-permute-start.8) | collective-permute-done | bytes 524320 | tf_op jit(solution)/shard_map/weight_z_near_late/ppermute | solution.py:51
  54.0 1.7 %collective-permute-start.9 = (bf16[4,256,512]{2,1,0:T(8,128)(2,1)S(1)}, bf16[4,256,512]{2,1,0:T(8,128)(2,1)}, u32[]{:S(2)}, u32[]{:S(2)}) collective-permute-start(bf16[4,256,512]{2,1,0:T(8,128)(2,1)S(1)} %constant_dynamic-update-slice_fusion.2.refs_2_), channel_id=1, source_target_pairs={{0,66},{1,65},{2,64},{3,67},{4,70},{5,69},{6,68},{7,71},{8,74},{9,... | collective-permute-start | bytes 3145736 | tf_op jit(solution)/shard_map/weight_z_back_late/ppermute | solution.py:51
  55.7 5.2 %forward.3.refs_6_ = f32[1024,512]{1,0:T(8,128)S(1)} custom-call(s32[5]{0:T(128)S(1)} %stack.23.refs_0_.at, bf16[1024,8192]{1,0:T(8,128)(2,1)} %refs_1_.5, bf16[4,256,512]{2,1,0:T(8,128)(2,1)} %constant_dynamic-update-slice_fusion.refs_2_, bf16[4,256,512]{2,1,0:T(8,128)(2,1)S(1)} %collective-permute-done.10.refs_3_), custom_call_target="tpu_custom_call" | custom-call | flops 12884901888 | bytes 1048576 | tf_op jit(solution)/shard_map/forward/pallas_call | solution.py:191
  61.5 0.8 copy-done.3
  62.5 1.7 %sums.1 = bf16[2,2,2,2,64,512]{5,4,3,2,1,0:T(8,128)(2,1)} custom-call(s32[5]{0:T(128)S(1)} %stack.23.refs_0_.at, f32[2,2,2,2,64,512]{5,4,3,2,1,0:T(8,128)S(1)} %copy.15.near_ref, bf16[2,2,2,64,512]{4,3,2,1,0:T(8,128)(2,1)S(1)} %collective-permute-done.12.near_in_ref, f32[2,2,2,2,64,512]{5,4,3,2,1,0:T(8,128)S(1)} %copy.16.far_ref, ...), custom_call_target="tpu_custom_call" | custom-call | tf_op jit(solution)/shard_map/sums/pallas_call | solution.py:239
  64.2 5.7 %all-to-all-start = ((bf16[16,64,512]{2,1,0:T(8,128)(2,1)}), bf16[16,64,512]{2,1,0:T(8,128)(2,1)S(1)}, u32[]{:S(2)}, u32[]{:S(2)}) async-start(bf16[16,64,512]{2,1,0:T(8,128)(2,1)} %bitcast.14), calls=%async_computation | async-start | bytes 2097152 | tf_op jit(solution)/shard_map/all_to_all | solution.py:299
  70.7 1.6 %copy-done.4 = f32[1024,512]{1,0:T(8,128)S(1)} copy-done((f32[1024,512]{1,0:T(8,128)S(1)}, f32[1024,512]{1,0:T(8,128)}, u32[]{:S(2)}) %copy-start.4) | copy-done | bytes 2097176
  72.3 8.3 %forward.4.refs_4_ = f32[1024,512]{1,0:T(8,128)S(1)} custom-call(s32[5]{0:T(128)S(1)} %stack.23.refs_0_.at, bf16[1024,8192]{1,0:T(8,128)(2,1)} %refs_1_.5, bf16[4,256,512]{2,1,0:T(8,128)(2,1)S(1)} %constant_dynamic-update-slice_fusion.2.refs_2_, bf16[4,256,512]{2,1,0:T(8,128)(2,1)} %collective-permute-done.7.refs_3_, ...), custom_call_target="tpu_custom_call" | custom-call | flops 17179869184 | bytes 1048576 | tf_op jit(solution)/shard_map/forward/pallas_call | solution.py:191
  80.7 6.0 %forward.5 = bf16[1024,512]{1,0:T(8,128)(2,1)} custom-call(s32[5]{0:T(128)S(1)} %stack.23.refs_0_.at, bf16[1024,8192]{1,0:T(8,128)(2,1)} %refs_1_.5, bf16[4,256,512]{2,1,0:T(8,128)(2,1)S(1)} %collective-permute-done.13.refs_2_, bf16[4,256,512]{2,1,0:T(8,128)(2,1)S(1)} %collective-permute-done.14.refs_3_, f32[1024,512]{1,0:T(8,128)S(1)} %forward.4.refs_4_, ...), custom_call_target="tpu_custom_call" | custom-call | flops 8589934592 | bytes 1048576 | tf_op jit(solution)/shard_map/forward/pallas_call | solution.py:191
  86.7 0.9 %total.1 = f32[64,512]{1,0:T(8,128)} custom-call(bf16[16,64,512]{2,1,0:T(8,128)(2,1)S(1)} %all-to-all-done.got_ref), custom_call_target="tpu_custom_call" | custom-call | tf_op jit(solution)/shard_map/total/pallas_call | solution.py:218
  (40 shorter events, 5.4 us)
Async XLA Ops:
  0.6 6.2 %copy-start = (bf16[1024,512]{1,0:T(8,128)(2,1)S(1)}, bf16[1024,512]{1,0:T(8,128)(2,1)}, u32[]{:S(2)}) copy-start(bf16[1024,512]{1,0:T(8,128)(2,1)} %cotangent_ref.1) | copy-start | bytes 3145732
  0.7 1.1 %copy-start.1 = (bf16[512,512]{1,0:T(8,128)(2,1)S(1)}, bf16[512,512]{1,0:T(8,128)(2,1)}, u32[]{:S(2)}) copy-start(bf16[512,512]{1,0:T(8,128)(2,1)} %codes_ref.1) | copy-start | bytes 1572868
  1.9 0.7 copy-start.2
  3.4 11.8 %collective-permute-start = (bf16[1,256,512]{2,1,0:T(8,128)(2,1)S(1)}, bf16[1,256,512]{2,1,0:T(8,128)(2,1)S(1)}, u32[]{:S(2)}, u32[]{:S(2)}) collective-permute-start(bf16[1,256,512]{2,1,0:T(8,128)(2,1)S(1)} %weight.1), channel_id=1, source_target_pairs={{0,4},{1,13},{2,6},{3,15},{4,0},{5,9},{6,2},{7,11},{8,12},{9,5},{1... | collective-permute-start | bytes 786440 | tf_op jit(solution)/shard_map/weight_y_near/ppermute | solution.py:51
  15.3 12.6 %collective-permute-start.3 = (bf16[2,256,512]{2,1,0:T(8,128)(2,1)S(1)}, bf16[2,256,512]{2,1,0:T(8,128)(2,1)S(1)}, u32[]{:S(2)}, u32[]{:S(2)}) collective-permute-start(bf16[2,256,512]{2,1,0:T(8,128)(2,1)S(1)} %pad_maximum_fusion), channel_id=1, source_target_pairs={{0,64},{1,67},{2,66},{3,65},{4,68},{5,71},{6,70},{7,69},{8,72},{9,... | collective-permute-start | bytes 1572872 | tf_op jit(solution)/shard_map/weight_z_near/ppermute | solution.py:51
  17.3 10.6 %collective-permute-start.2 = (bf16[2,256,512]{2,1,0:T(8,128)(2,1)S(1)}, bf16[2,256,512]{2,1,0:T(8,128)(2,1)S(1)}, u32[]{:S(2)}, u32[]{:S(2)}) collective-permute-start(bf16[2,256,512]{2,1,0:T(8,128)(2,1)S(1)} %pad_maximum_fusion), channel_id=1, source_target_pairs={{0,12},{1,5},{2,14},{3,7},{4,8},{5,1},{6,10},{7,3},{8,4},{9,13},{1... | collective-permute-start | bytes 1572872 | tf_op jit(solution)/shard_map/weight_y_back/ppermute | solution.py:51
  19.7 8.2 %collective-permute-start.1 = (bf16[2,2,2,2,2,64,512]{6,5,4,2,0,3,1:T(8,128)(2,1)S(1)}, bf16[2,2,2,2,2,64,512]{6,5,4,2,0,3,1:T(8,128)(2,1)S(1)}, u32[]{:S(2)}, u32[]{:S(2)}) collective-permute-start(bf16[2,2,2,2,2,64,512]{6,5,4,2,0,3,1:T(8,128)(2,1)S(1)} %copy.8), channel_id=1, source_target_pairs={{0,1},{1,0},{2,3},{3,2},{4,5},{5,4},{6,7},{7,6},{8,9},{9,8},{10,11... | collective-permute-start | bytes 6291464 | tf_op jit(solution)/shard_map/far_core/ppermute | solution.py:51
  28.1 4.4 %collective-permute-start.5 = (bf16[2,2,2,2,2,64,512]{6,5,4,2,0,1,3:T(8,128)(2,1)S(1)}, bf16[2,2,2,2,2,64,512]{6,5,4,2,0,1,3:T(8,128)(2,1)S(1)}, u32[]{:S(2)}, u32[]{:S(2)}) collective-permute-start(bf16[2,2,2,2,2,64,512]{6,5,4,2,0,1,3:T(8,128)(2,1)S(1)} %copy.11), channel_id=1, source_target_pairs={{0,1},{1,0},{2,3},{3,2},{4,5},{5,4},{6,7},{7,6},{8,9},{9,8},{10,11... | collective-permute-start | bytes 6291464 | tf_op jit(solution)/shard_map/near_core/ppermute | solution.py:51
  29.0 14.9 %collective-permute-start.4 = (bf16[2,2,2,2,64,512]{5,4,3,1,0,2:T(8,128)(2,1)S(1)}, bf16[2,2,2,2,64,512]{5,4,3,1,0,2:T(8,128)(2,1)S(1)}, u32[]{:S(2)}, u32[]{:S(2)}) collective-permute-start(bf16[2,2,2,2,64,512]{5,4,3,1,0,2:T(8,128)(2,1)S(1)} %fusion.6), channel_id=1, source_target_pairs={{0,16},{1,49},{2,18},{3,51},{4,20},{5,53},{6,22},{7,55},{8,24},{9,... | collective-permute-start | bytes 3145736 | tf_op jit(solution)/shard_map/far_x/ppermute | solution.py:51
  32.9 14.9 %collective-permute-start.6 = (bf16[2,2,2,2,64,512]{5,4,3,2,0,1:T(8,128)(2,1)S(1)}, bf16[2,2,2,2,64,512]{5,4,3,2,0,1:T(8,128)(2,1)S(1)}, u32[]{:S(2)}, u32[]{:S(2)}) collective-permute-start(bf16[2,2,2,2,64,512]{5,4,3,2,0,1:T(8,128)(2,1)S(1)} %fusion.7), channel_id=1, source_target_pairs={{0,4},{1,13},{2,6},{3,15},{4,0},{5,9},{6,2},{7,11},{8,12},{9,5},{1... | collective-permute-start | bytes 3145736 | tf_op jit(solution)/shard_map/near_y/ppermute | solution.py:51
  36.4 17.6 %collective-permute-start.10 = (bf16[4,256,512]{2,1,0:T(8,128)(2,1)}, bf16[4,256,512]{2,1,0:T(8,128)(2,1)S(1)}, u32[]{:S(2)}, u32[]{:S(2)}) collective-permute-start(bf16[4,256,512]{2,1,0:T(8,128)(2,1)} %constant_dynamic-update-slice_fusion.refs_2_), channel_id=1, source_target_pairs={{0,1},{1,0},{2,3},{3,2},{4,5},{5,4},{6,7},{7,6},{8,9},{9,8},{10,11... | collective-permute-start | bytes 3145736 | tf_op jit(solution)/shard_map/weight_core_0/ppermute | solution.py:51
  36.5 33.4 %collective-permute-start.7 = (bf16[4,256,512]{2,1,0:T(8,128)(2,1)}, bf16[4,256,512]{2,1,0:T(8,128)(2,1)}, u32[]{:S(2)}, u32[]{:S(2)}) collective-permute-start(bf16[4,256,512]{2,1,0:T(8,128)(2,1)} %constant_dynamic-update-slice_fusion.refs_2_), channel_id=1, source_target_pairs={{0,66},{1,65},{2,64},{3,67},{4,70},{5,69},{6,68},{7,71},{8,74},{9,... | collective-permute-start | bytes 3145736 | tf_op jit(solution)/shard_map/weight_z_back/ppermute | solution.py:51
  39.0 14.9 %collective-permute-start.8 = (bf16[2,256,512]{2,1,0:T(8,128)(2,1)S(1)}, bf16[2,256,512]{2,1,0:T(8,128)(2,1)S(1)}, u32[]{:S(2)}, u32[]{:S(2)}) collective-permute-start(bf16[2,256,512]{2,1,0:T(8,128)(2,1)S(1)} %collective-permute-done.2), channel_id=1, source_target_pairs={{0,64},{1,67},{2,66},{3,65},{4,68},{5,71},{6,70},{7,69},{8,72},{9,... | collective-permute-start | bytes 1572872 | tf_op jit(solution)/shard_map/weight_z_near_late/ppermute | solution.py:51
  44.8 17.6 %collective-permute-start.11 = (bf16[2,2,2,64,512]{4,3,2,1,0:T(8,128)(2,1)S(1)}, bf16[2,2,2,64,512]{4,3,2,1,0:T(8,128)(2,1)S(1)}, u32[]{:S(2)}, u32[]{:S(2)}) collective-permute-start(bf16[2,2,2,64,512]{4,3,2,1,0:T(8,128)(2,1)S(1)} %fusion.13), channel_id=1, source_target_pairs={{0,4},{1,13},{2,6},{3,15},{4,0},{5,9},{6,2},{7,11},{8,12},{9,5},{1... | collective-permute-start | bytes 1572872 | tf_op jit(solution)/shard_map/far_y/ppermute | solution.py:51
  48.0 14.5 %collective-permute-start.12 = (bf16[2,2,2,64,512]{4,3,2,1,0:T(8,128)(2,1)S(1)}, bf16[2,2,2,64,512]{4,3,2,1,0:T(8,128)(2,1)S(1)}, u32[]{:S(2)}, u32[]{:S(2)}) collective-permute-start(bf16[2,2,2,64,512]{4,3,2,1,0:T(8,128)(2,1)S(1)} %fusion.10), channel_id=1, source_target_pairs={{0,16},{1,49},{2,18},{3,51},{4,20},{5,53},{6,22},{7,55},{8,24},{9,... | collective-permute-start | bytes 1572872 | tf_op jit(solution)/shard_map/near_x/ppermute | solution.py:51
  53.9 16.8 %collective-permute-start.15 = (bf16[4,256,512]{2,1,0:T(8,128)(2,1)S(1)}, bf16[4,256,512]{2,1,0:T(8,128)(2,1)}, u32[]{:S(2)}, u32[]{:S(2)}) collective-permute-start(bf16[4,256,512]{2,1,0:T(8,128)(2,1)S(1)} %constant_dynamic-update-slice_fusion.2.refs_2_), channel_id=1, source_target_pairs={{0,1},{1,0},{2,3},{3,2},{4,5},{5,4},{6,7},{7,6},{8,9},{9,8},{10,11... | collective-permute-start | bytes 3145736 | tf_op jit(solution)/shard_map/weight_core_1/ppermute | solution.py:51
  54.0 16.2 %collective-permute-start.9 = (bf16[4,256,512]{2,1,0:T(8,128)(2,1)S(1)}, bf16[4,256,512]{2,1,0:T(8,128)(2,1)}, u32[]{:S(2)}, u32[]{:S(2)}) collective-permute-start(bf16[4,256,512]{2,1,0:T(8,128)(2,1)S(1)} %constant_dynamic-update-slice_fusion.2.refs_2_), channel_id=1, source_target_pairs={{0,66},{1,65},{2,64},{3,67},{4,70},{5,69},{6,68},{7,71},{8,74},{9,... | collective-permute-start | bytes 3145736 | tf_op jit(solution)/shard_map/weight_z_back_late/ppermute | solution.py:51
  61.0 1.3 %copy-start.3 = (f32[1024,512]{1,0:T(8,128)}, f32[1024,512]{1,0:T(8,128)S(1)}, u32[]{:S(2)}) copy-start(f32[1024,512]{1,0:T(8,128)S(1)} %forward.3.refs_6_) | copy-start | bytes 6291460
  64.2 22.5 %all-to-all-start = ((bf16[16,64,512]{2,1,0:T(8,128)(2,1)}), bf16[16,64,512]{2,1,0:T(8,128)(2,1)S(1)}, u32[]{:S(2)}, u32[]{:S(2)}) async-start(bf16[16,64,512]{2,1,0:T(8,128)(2,1)} %bitcast.14), calls=%async_computation | async-start | bytes 2097152 | tf_op jit(solution)/shard_map/all_to_all | solution.py:299
  70.2 10.4 %collective-permute-start.13 = (bf16[4,256,512]{2,1,0:T(8,128)(2,1)}, bf16[4,256,512]{2,1,0:T(8,128)(2,1)S(1)}, u32[]{:S(2)}, u32[]{:S(2)}) collective-permute-start(bf16[4,256,512]{2,1,0:T(8,128)(2,1)} %collective-permute-done.7.refs_3_), channel_id=1, source_target_pairs={{0,1},{1,0},{2,3},{3,2},{4,5},{5,4},{6,7},{7,6},{8,9},{9,8},{10,11... | collective-permute-start | bytes 3145736 | tf_op jit(solution)/shard_map/weight_core_2/ppermute | solution.py:51
  70.2 10.5 %collective-permute-start.14 = (bf16[4,256,512]{2,1,0:T(8,128)(2,1)}, bf16[4,256,512]{2,1,0:T(8,128)(2,1)S(1)}, u32[]{:S(2)}, u32[]{:S(2)}) collective-permute-start(bf16[4,256,512]{2,1,0:T(8,128)(2,1)} %collective-permute-done.9.refs_4_), channel_id=1, source_target_pairs={{0,1},{1,0},{2,3},{3,2},{4,5},{5,4},{6,7},{7,6},{8,9},{9,8},{10,11... | collective-permute-start | bytes 3145736 | tf_op jit(solution)/shard_map/weight_core_3/ppermute | solution.py:51
  70.7 1.6 %copy-start.4 = (f32[1024,512]{1,0:T(8,128)S(1)}, f32[1024,512]{1,0:T(8,128)}, u32[]{:S(2)}) copy-start(f32[1024,512]{1,0:T(8,128)} %copy-done.3) | copy-start | bytes 6291460

commit v4 on v3

--- a/solution.py
+++ b/solution.py
@@ -292,7 +292,7 @@
     sib += [send("weight_core_1", parts[1], core=(1, 1))]
     at, _, _ = tie((at, far_sent, near_sent))
     half = forward(
-        at, tokens, [(0, 0, 0, 0, 0), (0, 0, 1, 1, 0)], [parts[0], sib[0]], cover=24
+        at, tokens, [(0, 0, 0, 0, 0)], [parts[0]], cover=24
     )
     half, far_in, near_in = tie((half, far_in, near_in))
     mine = sums(at, near, near_in, far, far_in).reshape(16, 64, 512)
@@ -302,8 +302,8 @@
     half = forward(
         at,
         tokens,
-        [(0, 1, 0, 0, 0), (1, 0, 0, 1, 0), (1, 1, 0, 2, 0), (0, 1, 1, 3, 0)],
-        [parts[1], late[0], late[1], sib[1]],
+        [(0, 1, 0, 0, 0), (1, 0, 0, 1, 0), (1, 1, 0, 2, 0), (0, 0, 1, 4, 0), (0, 1, 1, 3, 0)],
+        [parts[1], late[0], late[1], sib[1], sib[0]],
         half,
         cover=32,
     )

time: 89.1 us -> 90.6 us (1.017)
  no operation moved by 1% of the time
where the time goes in v4:
time: 90.6 us; the launch traced here: 89.3 us
  Pallas kernels  39.2 us (43%)
  starting transfers between devices  25.9 us (29%)
  waiting for transfers between devices  12.3 us (14%)
  local copies, waits for them, and re-layouts  6.86 us (8%)
  other arithmetic  3.9 us (4%)
  between operations  1.1 us (1%)
    pallas_call x3, Pallas kernels, forward(): pl.pallas_call(lambda *refs: forward_kernel(parts, len(weights), *refs),...  19.9 us
    ppermute x16, starting transfers between devices, send(): return lax.ppermute(value, BITS, pairs)  19.6 us
    pallas_call x2, Pallas kernels, grad_half(): pl.pallas_call(lambda *refs: grad_kernel(chunk, *refs), in_specs=[SCALAR,...  14.9 us
    ppermute x16, waiting for transfers between devices, send(): return lax.ppermute(value, BITS, pairs)  12.3 us
    all_to_all x1, starting transfers between devices, local(): lax.all_to_all(mine, BITS, 0, 0, axis_index_groups=quads(), tiled=True)  6.26 us
    unnamed x12, local copies, waits for them, and re-layouts  5.1 us
  transfers between devices with their start and end apart: 17, of which 5 were waited for; matrix products, arithmetic and copies ran while one was open for 7% of the time, Pallas kernels for 42%

profile of v4, /device:TPU:0, one launch (start us, length us, event | category | flops | bytes accessed | tf_op | source)
XLA Modules:
  0.0 89.3 jit_solution(9253067096516795524)
XLA Ops:
  0.7 1.1 %copy-done.1 = bf16[512,512]{1,0:T(8,128)(2,1)S(1)} copy-done((bf16[512,512]{1,0:T(8,128)(2,1)S(1)}, bf16[512,512]{1,0:T(8,128)(2,1)}, u32[]{:S(2)}) %copy-start.1) | copy-done | bytes 524312
  2.5 0.9 weight.1
  3.4 1.7 %collective-permute-start = (bf16[1,256,512]{2,1,0:T(8,128)(2,1)S(1)}, bf16[1,256,512]{2,1,0:T(8,128)(2,1)S(1)}, u32[]{:S(2)}, u32[]{:S(2)}) collective-permute-start(bf16[1,256,512]{2,1,0:T(8,128)(2,1)S(1)} %weight.1), channel_id=1, source_target_pairs={{0,4},{1,13},{2,6},{3,15},{4,0},{5,9},{6,2},{7,11},{8,12},{9,5},{1... | collective-permute-start | bytes 786440 | tf_op jit(solution)/shard_map/weight_y_near/ppermute | solution.py:51
  5.9 1.0 %multiply_sine_fusion = (f32[64,1024]{1,0:T(8,128)S(1)}, f32[64,1024]{1,0:T(8,128)S(1)}) fusion(f32[1024]{0:T(1024)S(1)} %convert_element_type.63, f32[64]{0:T(128)S(1)} %multiply_power_fusion), kind=kLoop, calls=%fused_computation.23 | loop fusion | flops 65536 | bytes 528640 | tf_op jit(solution)/shard_map/sin | solution.py:259
  6.9 0.9 back.1.refs_1_
  7.8 7.5 %grad.2 = (f32[2,2,2,2,2,64,512]{6,5,4,3,2,1,0:T(8,128)S(1)}, bf16[2,2,2,2,2,64,512]{6,5,4,3,2,1,0:T(8,128)(2,1)S(1)}) custom-call(s32[5]{0:T(128)S(1)} %stack.23.refs_0_.at, bf16[1024,512]{1,0:T(8,128)(2,1)S(1)} %back.1.refs_1_, bf16[1024,8192]{1,0:T(8,128)(2,1)} %refs_1_.5), custom_call_target="tpu_custom_call" | custom-call | flops 42949672960 | bytes 8388608 | tf_op jit(solution)/shard_map/grad/pallas_call | solution.py:133
  15.3 2.0 %collective-permute-start.3 = (bf16[2,256,512]{2,1,0:T(8,128)(2,1)S(1)}, bf16[2,256,512]{2,1,0:T(8,128)(2,1)S(1)}, u32[]{:S(2)}, u32[]{:S(2)}) collective-permute-start(bf16[2,256,512]{2,1,0:T(8,128)(2,1)S(1)} %pad_maximum_fusion), channel_id=1, source_target_pairs={{0,64},{1,67},{2,66},{3,65},{4,68},{5,71},{6,70},{7,69},{8,72},{9,... | collective-permute-start | bytes 1572872 | tf_op jit(solution)/shard_map/weight_z_near/ppermute | solution.py:51
  17.3 2.2 %collective-permute-start.2 = (bf16[2,256,512]{2,1,0:T(8,128)(2,1)S(1)}, bf16[2,256,512]{2,1,0:T(8,128)(2,1)S(1)}, u32[]{:S(2)}, u32[]{:S(2)}) collective-permute-start(bf16[2,256,512]{2,1,0:T(8,128)(2,1)S(1)} %pad_maximum_fusion), channel_id=1, source_target_pairs={{0,12},{1,5},{2,14},{3,7},{4,8},{5,1},{6,10},{7,3},{8,4},{9,13},{1... | collective-permute-start | bytes 1572872 | tf_op jit(solution)/shard_map/weight_y_back/ppermute | solution.py:51
  19.7 0.7 collective-permute-start.1
  20.4 7.5 %grad.3 = (f32[2,2,2,2,2,64,512]{6,5,4,3,2,1,0:T(8,128)S(1)}, bf16[2,2,2,2,2,64,512]{6,5,4,3,2,1,0:T(8,128)(2,1)S(1)}) custom-call(s32[5]{0:T(128)S(1)} %stack.23.refs_0_.at, bf16[1024,512]{1,0:T(8,128)(2,1)S(1)} %back.1.refs_1_, bf16[1024,8192]{1,0:T(8,128)(2,1)} %refs_1_.5), custom_call_target="tpu_custom_call" | custom-call | flops 42949672960 | bytes 8388608 | tf_op jit(solution)/shard_map/grad/pallas_call | solution.py:133
  29.0 1.6 %collective-permute-start.4 = (bf16[2,2,2,2,64,512]{5,4,3,1,0,2:T(8,128)(2,1)S(1)}, bf16[2,2,2,2,64,512]{5,4,3,1,0,2:T(8,128)(2,1)S(1)}, u32[]{:S(2)}, u32[]{:S(2)}) collective-permute-start(bf16[2,2,2,2,64,512]{5,4,3,1,0,2:T(8,128)(2,1)S(1)} %fusion.6), channel_id=1, source_target_pairs={{0,16},{1,49},{2,18},{3,51},{4,20},{5,53},{6,22},{7,55},{8,24},{9,... | collective-permute-start | bytes 3145736 | tf_op jit(solution)/shard_map/far_x/ppermute | solution.py:51
  30.6 2.0 %collective-permute-done.5 = bf16[2,2,2,2,2,64,512]{6,5,4,2,0,1,3:T(8,128)(2,1)S(1)} collective-permute-done((bf16[2,2,2,2,2,64,512]{6,5,4,2,0,1,3:T(8,128)(2,1)S(1)}, bf16[2,2,2,2,2,64,512]{6,5,4,2,0,1,3:T(8,128)(2,1)S(1)}, u32[]{:S(2)}, u32[]{:S(2)}) %collective-permute-start.5) | collective-permute-done | bytes 2097184 | tf_op jit(solution)/shard_map/near_core/ppermute | solution.py:51
  32.9 1.8 %collective-permute-start.6 = (bf16[2,2,2,2,64,512]{5,4,3,2,0,1:T(8,128)(2,1)S(1)}, bf16[2,2,2,2,64,512]{5,4,3,2,0,1:T(8,128)(2,1)S(1)}, u32[]{:S(2)}, u32[]{:S(2)}) collective-permute-start(bf16[2,2,2,2,64,512]{5,4,3,2,0,1:T(8,128)(2,1)S(1)} %fusion.7), channel_id=1, source_target_pairs={{0,4},{1,13},{2,6},{3,15},{4,0},{5,9},{6,2},{7,11},{8,12},{9,5},{1... | collective-permute-start | bytes 3145736 | tf_op jit(solution)/shard_map/near_y/ppermute | solution.py:51
  34.7 0.8 constant_dynamic-update-slice_fusion.1
  35.6 0.8 constant_dynamic-update-slice_fusion.refs_2_
  36.5 2.5 %collective-permute-start.7 = (bf16[4,256,512]{2,1,0:T(8,128)(2,1)}, bf16[4,256,512]{2,1,0:T(8,128)(2,1)}, u32[]{:S(2)}, u32[]{:S(2)}) collective-permute-start(bf16[4,256,512]{2,1,0:T(8,128)(2,1)} %constant_dynamic-update-slice_fusion.refs_2_), channel_id=1, source_target_pairs={{0,66},{1,65},{2,64},{3,67},{4,70},{5,69},{6,68},{7,71},{8,74},{9,... | collective-permute-start | bytes 3145736 | tf_op jit(solution)/shard_map/weight_z_back/ppermute | solution.py:51
  39.0 1.0 %collective-permute-start.8 = (bf16[2,256,512]{2,1,0:T(8,128)(2,1)S(1)}, bf16[2,256,512]{2,1,0:T(8,128)(2,1)S(1)}, u32[]{:S(2)}, u32[]{:S(2)}) collective-permute-start(bf16[2,256,512]{2,1,0:T(8,128)(2,1)S(1)} %collective-permute-done.2), channel_id=1, source_target_pairs={{0,64},{1,67},{2,66},{3,65},{4,68},{5,71},{6,70},{7,69},{8,72},{9,... | collective-permute-start | bytes 1572872 | tf_op jit(solution)/shard_map/weight_z_near_late/ppermute | solution.py:51
  40.1 3.8 %collective-permute-done.4 = bf16[2,2,2,2,64,512]{5,4,3,1,0,2:T(8,128)(2,1)S(1)} collective-permute-done((bf16[2,2,2,2,64,512]{5,4,3,1,0,2:T(8,128)(2,1)S(1)}, bf16[2,2,2,2,64,512]{5,4,3,1,0,2:T(8,128)(2,1)S(1)}, u32[]{:S(2)}, u32[]{:S(2)}) %collective-permute-start.4) | collective-permute-done | bytes 1048608 | tf_op jit(solution)/shard_map/far_x/ppermute | solution.py:51
  44.1 1.6 %collective-permute-start.10 = (bf16[2,2,2,64,512]{4,3,2,1,0:T(8,128)(2,1)S(1)}, bf16[2,2,2,64,512]{4,3,2,1,0:T(8,128)(2,1)S(1)}, u32[]{:S(2)}, u32[]{:S(2)}) collective-permute-start(bf16[2,2,2,64,512]{4,3,2,1,0:T(8,128)(2,1)S(1)} %fusion.13), channel_id=1, source_target_pairs={{0,4},{1,13},{2,6},{3,15},{4,0},{5,9},{6,2},{7,11},{8,12},{9,5},{1... | collective-permute-start | bytes 1572872 | tf_op jit(solution)/shard_map/far_y/ppermute | solution.py:51
  46.4 1.4 %collective-permute-done.6 = bf16[2,2,2,2,64,512]{5,4,3,2,0,1:T(8,128)(2,1)S(1)} collective-permute-done((bf16[2,2,2,2,64,512]{5,4,3,2,0,1:T(8,128)(2,1)S(1)}, bf16[2,2,2,2,64,512]{5,4,3,2,0,1:T(8,128)(2,1)S(1)}, u32[]{:S(2)}, u32[]{:S(2)}) %collective-permute-start.6) | collective-permute-done | bytes 1048608 | tf_op jit(solution)/shard_map/near_y/ppermute | solution.py:51
  48.0 1.6 %collective-permute-start.11 = (bf16[2,2,2,64,512]{4,3,2,1,0:T(8,128)(2,1)S(1)}, bf16[2,2,2,64,512]{4,3,2,1,0:T(8,128)(2,1)S(1)}, u32[]{:S(2)}, u32[]{:S(2)}) collective-permute-start(bf16[2,2,2,64,512]{4,3,2,1,0:T(8,128)(2,1)S(1)} %fusion.10), channel_id=1, source_target_pairs={{0,16},{1,49},{2,18},{3,51},{4,20},{5,53},{6,22},{7,55},{8,24},{9,... | collective-permute-start | bytes 1572872 | tf_op jit(solution)/shard_map/near_x/ppermute | solution.py:51
  49.6 4.2 %collective-permute-done.8 = bf16[2,256,512]{2,1,0:T(8,128)(2,1)S(1)} collective-permute-done((bf16[2,256,512]{2,1,0:T(8,128)(2,1)S(1)}, bf16[2,256,512]{2,1,0:T(8,128)(2,1)S(1)}, u32[]{:S(2)}, u32[]{:S(2)}) %collective-permute-start.8) | collective-permute-done | bytes 524320 | tf_op jit(solution)/shard_map/weight_z_near_late/ppermute | solution.py:51
  54.0 1.7 %collective-permute-start.9 = (bf16[4,256,512]{2,1,0:T(8,128)(2,1)S(1)}, bf16[4,256,512]{2,1,0:T(8,128)(2,1)}, u32[]{:S(2)}, u32[]{:S(2)}) collective-permute-start(bf16[4,256,512]{2,1,0:T(8,128)(2,1)S(1)} %constant_dynamic-update-slice_fusion.2.refs_2_), channel_id=1, source_target_pairs={{0,66},{1,65},{2,64},{3,67},{4,70},{5,69},{6,68},{7,71},{8,74},{9,... | collective-permute-start | bytes 3145736 | tf_op jit(solution)/shard_map/weight_z_back_late/ppermute | solution.py:51
  55.7 4.1 %forward.3.refs_7_ = f32[1024,512]{1,0:T(8,128)S(1)} custom-call(s32[5]{0:T(128)S(1)} %stack.23.refs_0_.at, bf16[1024,8192]{1,0:T(8,128)(2,1)} %refs_1_.5, bf16[4,256,512]{2,1,0:T(8,128)(2,1)} %constant_dynamic-update-slice_fusion.refs_2_), custom_call_target="tpu_custom_call" | custom-call | flops 12884901888 | bytes 1048576 | tf_op jit(solution)/shard_map/forward/pallas_call | solution.py:191
  60.3 0.8 copy-done.3
  61.3 1.7 %sums.1 = bf16[2,2,2,2,64,512]{5,4,3,2,1,0:T(8,128)(2,1)} custom-call(s32[5]{0:T(128)S(1)} %stack.23.refs_0_.at, f32[2,2,2,2,64,512]{5,4,3,2,1,0:T(8,128)S(1)} %copy.15.near_ref, bf16[2,2,2,64,512]{4,3,2,1,0:T(8,128)(2,1)S(1)} %collective-permute-done.11.near_in_ref, f32[2,2,2,2,64,512]{5,4,3,2,1,0:T(8,128)S(1)} %copy.16.far_ref, ...), custom_call_target="tpu_custom_call" | custom-call | tf_op jit(solution)/shard_map/sums/pallas_call | solution.py:239
  63.0 6.3 %all-to-all-start = ((bf16[16,64,512]{2,1,0:T(8,128)(2,1)}), bf16[16,64,512]{2,1,0:T(8,128)(2,1)S(1)}, u32[]{:S(2)}, u32[]{:S(2)}) async-start(bf16[16,64,512]{2,1,0:T(8,128)(2,1)} %bitcast.14), calls=%async_computation | async-start | bytes 2097152 | tf_op jit(solution)/shard_map/all_to_all | solution.py:299
  69.3 0.9 %collective-permute-done.9.refs_4_ = bf16[4,256,512]{2,1,0:T(8,128)(2,1)} collective-permute-done((bf16[4,256,512]{2,1,0:T(8,128)(2,1)S(1)}, bf16[4,256,512]{2,1,0:T(8,128)(2,1)}, u32[]{:S(2)}, u32[]{:S(2)}) %collective-permute-start.9) | collective-permute-done | bytes 1048608 | tf_op jit(solution)/shard_map/weight_z_back_late/ppermute | solution.py:51
  70.7 1.6 %copy-done.4 = f32[1024,512]{1,0:T(8,128)S(1)} copy-done((f32[1024,512]{1,0:T(8,128)S(1)}, f32[1024,512]{1,0:T(8,128)}, u32[]{:S(2)}) %copy-start.4) | copy-done | bytes 2097176
  72.3 9.8 %forward.4.refs_4_ = f32[1024,512]{1,0:T(8,128)S(1)} custom-call(s32[5]{0:T(128)S(1)} %stack.23.refs_0_.at, bf16[1024,8192]{1,0:T(8,128)(2,1)} %refs_1_.5, bf16[4,256,512]{2,1,0:T(8,128)(2,1)S(1)} %constant_dynamic-update-slice_fusion.2.refs_2_, bf16[4,256,512]{2,1,0:T(8,128)(2,1)} %collective-permute-done.7.refs_3_, ...), custom_call_target="tpu_custom_call" | custom-call | flops 17179869184 | bytes 1048576 | tf_op jit(solution)/shard_map/forward/pallas_call | solution.py:191
  82.2 6.0 %forward.5 = bf16[1024,512]{1,0:T(8,128)(2,1)} custom-call(s32[5]{0:T(128)S(1)} %stack.23.refs_0_.at, bf16[1024,8192]{1,0:T(8,128)(2,1)} %refs_1_.5, bf16[4,256,512]{2,1,0:T(8,128)(2,1)S(1)} %collective-permute-done.12.refs_2_, bf16[4,256,512]{2,1,0:T(8,128)(2,1)S(1)} %collective-permute-done.13.refs_3_, f32[1024,512]{1,0:T(8,128)S(1)} %forward.4.refs_4_, ...), custom_call_target="tpu_custom_call" | custom-call | flops 8589934592 | bytes 1048576 | tf_op jit(solution)/shard_map/forward/pallas_call | solution.py:191
  88.2 0.9 %total.1 = f32[64,512]{1,0:T(8,128)} custom-call(bf16[16,64,512]{2,1,0:T(8,128)(2,1)S(1)} %all-to-all-done.got_ref), custom_call_target="tpu_custom_call" | custom-call | tf_op jit(solution)/shard_map/total/pallas_call | solution.py:218
  (40 shorter events, 5.8 us)
Async XLA Ops:
  0.6 6.2 %copy-start = (bf16[1024,512]{1,0:T(8,128)(2,1)S(1)}, bf16[1024,512]{1,0:T(8,128)(2,1)}, u32[]{:S(2)}) copy-start(bf16[1024,512]{1,0:T(8,128)(2,1)} %cotangent_ref.1) | copy-start | bytes 3145732
  0.7 1.1 %copy-start.1 = (bf16[512,512]{1,0:T(8,128)(2,1)S(1)}, bf16[512,512]{1,0:T(8,128)(2,1)}, u32[]{:S(2)}) copy-start(bf16[512,512]{1,0:T(8,128)(2,1)} %codes_ref.1) | copy-start | bytes 1572868
  1.9 0.7 copy-start.2
  3.4 11.8 %collective-permute-start = (bf16[1,256,512]{2,1,0:T(8,128)(2,1)S(1)}, bf16[1,256,512]{2,1,0:T(8,128)(2,1)S(1)}, u32[]{:S(2)}, u32[]{:S(2)}) collective-permute-start(bf16[1,256,512]{2,1,0:T(8,128)(2,1)S(1)} %weight.1), channel_id=1, source_target_pairs={{0,4},{1,13},{2,6},{3,15},{4,0},{5,9},{6,2},{7,11},{8,12},{9,5},{1... | collective-permute-start | bytes 786440 | tf_op jit(solution)/shard_map/weight_y_near/ppermute | solution.py:51
  15.3 12.6 %collective-permute-start.3 = (bf16[2,256,512]{2,1,0:T(8,128)(2,1)S(1)}, bf16[2,256,512]{2,1,0:T(8,128)(2,1)S(1)}, u32[]{:S(2)}, u32[]{:S(2)}) collective-permute-start(bf16[2,256,512]{2,1,0:T(8,128)(2,1)S(1)} %pad_maximum_fusion), channel_id=1, source_target_pairs={{0,64},{1,67},{2,66},{3,65},{4,68},{5,71},{6,70},{7,69},{8,72},{9,... | collective-permute-start | bytes 1572872 | tf_op jit(solution)/shard_map/weight_z_near/ppermute | solution.py:51
  17.3 10.6 %collective-permute-start.2 = (bf16[2,256,512]{2,1,0:T(8,128)(2,1)S(1)}, bf16[2,256,512]{2,1,0:T(8,128)(2,1)S(1)}, u32[]{:S(2)}, u32[]{:S(2)}) collective-permute-start(bf16[2,256,512]{2,1,0:T(8,128)(2,1)S(1)} %pad_maximum_fusion), channel_id=1, source_target_pairs={{0,12},{1,5},{2,14},{3,7},{4,8},{5,1},{6,10},{7,3},{8,4},{9,13},{1... | collective-permute-start | bytes 1572872 | tf_op jit(solution)/shard_map/weight_y_back/ppermute | solution.py:51
  19.7 8.2 %collective-permute-start.1 = (bf16[2,2,2,2,2,64,512]{6,5,4,2,0,3,1:T(8,128)(2,1)S(1)}, bf16[2,2,2,2,2,64,512]{6,5,4,2,0,3,1:T(8,128)(2,1)S(1)}, u32[]{:S(2)}, u32[]{:S(2)}) collective-permute-start(bf16[2,2,2,2,2,64,512]{6,5,4,2,0,3,1:T(8,128)(2,1)S(1)} %copy.8), channel_id=1, source_target_pairs={{0,1},{1,0},{2,3},{3,2},{4,5},{5,4},{6,7},{7,6},{8,9},{9,8},{10,11... | collective-permute-start | bytes 6291464 | tf_op jit(solution)/shard_map/far_core/ppermute | solution.py:51
  28.1 4.4 %collective-permute-start.5 = (bf16[2,2,2,2,2,64,512]{6,5,4,2,0,1,3:T(8,128)(2,1)S(1)}, bf16[2,2,2,2,2,64,512]{6,5,4,2,0,1,3:T(8,128)(2,1)S(1)}, u32[]{:S(2)}, u32[]{:S(2)}) collective-permute-start(bf16[2,2,2,2,2,64,512]{6,5,4,2,0,1,3:T(8,128)(2,1)S(1)} %copy.11), channel_id=1, source_target_pairs={{0,1},{1,0},{2,3},{3,2},{4,5},{5,4},{6,7},{7,6},{8,9},{9,8},{10,11... | collective-permute-start | bytes 6291464 | tf_op jit(solution)/shard_map/near_core/ppermute | solution.py:51
  29.0 14.9 %collective-permute-start.4 = (bf16[2,2,2,2,64,512]{5,4,3,1,0,2:T(8,128)(2,1)S(1)}, bf16[2,2,2,2,64,512]{5,4,3,1,0,2:T(8,128)(2,1)S(1)}, u32[]{:S(2)}, u32[]{:S(2)}) collective-permute-start(bf16[2,2,2,2,64,512]{5,4,3,1,0,2:T(8,128)(2,1)S(1)} %fusion.6), channel_id=1, source_target_pairs={{0,16},{1,49},{2,18},{3,51},{4,20},{5,53},{6,22},{7,55},{8,24},{9,... | collective-permute-start | bytes 3145736 | tf_op jit(solution)/shard_map/far_x/ppermute | solution.py:51
  32.9 14.9 %collective-permute-start.6 = (bf16[2,2,2,2,64,512]{5,4,3,2,0,1:T(8,128)(2,1)S(1)}, bf16[2,2,2,2,64,512]{5,4,3,2,0,1:T(8,128)(2,1)S(1)}, u32[]{:S(2)}, u32[]{:S(2)}) collective-permute-start(bf16[2,2,2,2,64,512]{5,4,3,2,0,1:T(8,128)(2,1)S(1)} %fusion.7), channel_id=1, source_target_pairs={{0,4},{1,13},{2,6},{3,15},{4,0},{5,9},{6,2},{7,11},{8,12},{9,5},{1... | collective-permute-start | bytes 3145736 | tf_op jit(solution)/shard_map/near_y/ppermute | solution.py:51
  36.4 34.3 %collective-permute-start.15 = (bf16[4,256,512]{2,1,0:T(8,128)(2,1)}, bf16[4,256,512]{2,1,0:T(8,128)(2,1)}, u32[]{:S(2)}, u32[]{:S(2)}) collective-permute-start(bf16[4,256,512]{2,1,0:T(8,128)(2,1)} %constant_dynamic-update-slice_fusion.refs_2_), channel_id=1, source_target_pairs={{0,1},{1,0},{2,3},{3,2},{4,5},{5,4},{6,7},{7,6},{8,9},{9,8},{10,11... | collective-permute-start | bytes 3145736 | tf_op jit(solution)/shard_map/weight_core_0/ppermute | solution.py:51
  36.5 32.8 %collective-permute-start.7 = (bf16[4,256,512]{2,1,0:T(8,128)(2,1)}, bf16[4,256,512]{2,1,0:T(8,128)(2,1)}, u32[]{:S(2)}, u32[]{:S(2)}) collective-permute-start(bf16[4,256,512]{2,1,0:T(8,128)(2,1)} %constant_dynamic-update-slice_fusion.refs_2_), channel_id=1, source_target_pairs={{0,66},{1,65},{2,64},{3,67},{4,70},{5,69},{6,68},{7,71},{8,74},{9,... | collective-permute-start | bytes 3145736 | tf_op jit(solution)/shard_map/weight_z_back/ppermute | solution.py:51
  39.0 14.9 %collective-permute-start.8 = (bf16[2,256,512]{2,1,0:T(8,128)(2,1)S(1)}, bf16[2,256,512]{2,1,0:T(8,128)(2,1)S(1)}, u32[]{:S(2)}, u32[]{:S(2)}) collective-permute-start(bf16[2,256,512]{2,1,0:T(8,128)(2,1)S(1)} %collective-permute-done.2), channel_id=1, source_target_pairs={{0,64},{1,67},{2,66},{3,65},{4,68},{5,71},{6,70},{7,69},{8,72},{9,... | collective-permute-start | bytes 1572872 | tf_op jit(solution)/shard_map/weight_z_near_late/ppermute | solution.py:51
  44.1 9.9 %collective-permute-start.10 = (bf16[2,2,2,64,512]{4,3,2,1,0:T(8,128)(2,1)S(1)}, bf16[2,2,2,64,512]{4,3,2,1,0:T(8,128)(2,1)S(1)}, u32[]{:S(2)}, u32[]{:S(2)}) collective-permute-start(bf16[2,2,2,64,512]{4,3,2,1,0:T(8,128)(2,1)S(1)} %fusion.13), channel_id=1, source_target_pairs={{0,4},{1,13},{2,6},{3,15},{4,0},{5,9},{6,2},{7,11},{8,12},{9,5},{1... | collective-permute-start | bytes 1572872 | tf_op jit(solution)/shard_map/far_y/ppermute | solution.py:51
  48.0 13.3 %collective-permute-start.11 = (bf16[2,2,2,64,512]{4,3,2,1,0:T(8,128)(2,1)S(1)}, bf16[2,2,2,64,512]{4,3,2,1,0:T(8,128)(2,1)S(1)}, u32[]{:S(2)}, u32[]{:S(2)}) collective-permute-start(bf16[2,2,2,64,512]{4,3,2,1,0:T(8,128)(2,1)S(1)} %fusion.10), channel_id=1, source_target_pairs={{0,16},{1,49},{2,18},{3,51},{4,20},{5,53},{6,22},{7,55},{8,24},{9,... | collective-permute-start | bytes 1572872 | tf_op jit(solution)/shard_map/near_x/ppermute | solution.py:51
  53.9 16.8 %collective-permute-start.14 = (bf16[4,256,512]{2,1,0:T(8,128)(2,1)S(1)}, bf16[4,256,512]{2,1,0:T(8,128)(2,1)}, u32[]{:S(2)}, u32[]{:S(2)}) collective-permute-start(bf16[4,256,512]{2,1,0:T(8,128)(2,1)S(1)} %constant_dynamic-update-slice_fusion.2.refs_2_), channel_id=1, source_target_pairs={{0,1},{1,0},{2,3},{3,2},{4,5},{5,4},{6,7},{7,6},{8,9},{9,8},{10,11... | collective-permute-start | bytes 3145736 | tf_op jit(solution)/shard_map/weight_core_1/ppermute | solution.py:51
  54.0 16.2 %collective-permute-start.9 = (bf16[4,256,512]{2,1,0:T(8,128)(2,1)S(1)}, bf16[4,256,512]{2,1,0:T(8,128)(2,1)}, u32[]{:S(2)}, u32[]{:S(2)}) collective-permute-start(bf16[4,256,512]{2,1,0:T(8,128)(2,1)S(1)} %constant_dynamic-update-slice_fusion.2.refs_2_), channel_id=1, source_target_pairs={{0,66},{1,65},{2,64},{3,67},{4,70},{5,69},{6,68},{7,71},{8,74},{9,... | collective-permute-start | bytes 3145736 | tf_op jit(solution)/shard_map/weight_z_back_late/ppermute | solution.py:51
  59.8 1.3 %copy-start.3 = (f32[1024,512]{1,0:T(8,128)}, f32[1024,512]{1,0:T(8,128)S(1)}, u32[]{:S(2)}) copy-start(f32[1024,512]{1,0:T(8,128)S(1)} %forward.3.refs_7_) | copy-start | bytes 6291460
  63.0 25.1 %all-to-all-start = ((bf16[16,64,512]{2,1,0:T(8,128)(2,1)}), bf16[16,64,512]{2,1,0:T(8,128)(2,1)S(1)}, u32[]{:S(2)}, u32[]{:S(2)}) async-start(bf16[16,64,512]{2,1,0:T(8,128)(2,1)} %bitcast.14), calls=%async_computation | async-start | bytes 2097152 | tf_op jit(solution)/shard_map/all_to_all | solution.py:299
  70.2 11.9 %collective-permute-start.12 = (bf16[4,256,512]{2,1,0:T(8,128)(2,1)}, bf16[4,256,512]{2,1,0:T(8,128)(2,1)S(1)}, u32[]{:S(2)}, u32[]{:S(2)}) collective-permute-start(bf16[4,256,512]{2,1,0:T(8,128)(2,1)} %collective-permute-done.7.refs_3_), channel_id=1, source_target_pairs={{0,1},{1,0},{2,3},{3,2},{4,5},{5,4},{6,7},{7,6},{8,9},{9,8},{10,11... | collective-permute-start | bytes 3145736 | tf_op jit(solution)/shard_map/weight_core_2/ppermute | solution.py:51
  70.2 11.9 %collective-permute-start.13 = (bf16[4,256,512]{2,1,0:T(8,128)(2,1)}, bf16[4,256,512]{2,1,0:T(8,128)(2,1)S(1)}, u32[]{:S(2)}, u32[]{:S(2)}) collective-permute-start(bf16[4,256,512]{2,1,0:T(8,128)(2,1)} %collective-permute-done.9.refs_4_), channel_id=1, source_target_pairs={{0,1},{1,0},{2,3},{3,2},{4,5},{5,4},{6,7},{7,6},{8,9},{9,8},{10,11... | collective-permute-start | bytes 3145736 | tf_op jit(solution)/shard_map/weight_core_3/ppermute | solution.py:51
  70.7 1.6 %copy-start.4 = (f32[1024,512]{1,0:T(8,128)S(1)}, f32[1024,512]{1,0:T(8,128)}, u32[]{:S(2)}) copy-start(f32[1024,512]{1,0:T(8,128)} %copy-done.3) | copy-start | bytes 6291460
